TPU v7x, 32 devices: a whole 2x2x4 slice. The times are simulated.
32 devices in a mesh: rows: 8 (over z, core), batch: 4 (over y, x).
Axes of the slice: x: 2, y: 2, z: 4, core: 2. Of those that a mesh axis runs over, the one named last changes fastest.
Arguments:
- inputs: bfloat16 [32, 32, 32, 512], P('batch', 'rows')
- counts: int32 [4], P('batch'), may hold values from 2 to 8, as said below
- down_weight: bfloat16 [3, 3, 512, 1024], replicated, may hold values from -0.09375 to 0.09375
- left_weight: bfloat16 [1024, 512], replicated, may hold values from -0.1875 to 0.1875
- right_weight: bfloat16 [1024, 512], replicated, may hold values from -0.1875 to 0.1875
- reduce_weight: bfloat16 [512, 512], replicated, may hold values from -0.25 to 0.25
- spread_weight: bfloat16 [3, 3, 512, 512], replicated, may hold values from -0.09375 to 0.09375
- norm_gains: float32 [3072], replicated, may hold values from 0.5 to 1.5
- norm_biases: float32 [3072], replicated, may hold values from -1.5 to 1.5
- running_mean: float32 [3072], replicated, may hold values from -1.5 to 1.5
- running_var: float32 [3072], replicated, may hold values from 0.5 to 2
- section_cotangent: bfloat16 [32, 16, 16, 1024], P('batch', 'rows'), may hold values from -6 to 6
- block_cotangent: bfloat16 [32, 16, 16, 512], P('batch', 'rows'), may hold values from -6 to 6
Outputs:
- section_out: bfloat16 [32, 16, 16, 1024], P('batch', 'rows')
- block_out: bfloat16 [32, 16, 16, 512], P('batch', 'rows')
- input_grad: bfloat16 [32, 32, 32, 512], P('batch', 'rows')
- weight_grads: float32 [8388608], P(('rows', 'batch'))
- gain_grads: float32 [3072], replicated
- bias_grads: float32 [3072], replicated
- new_mean: float32 [3072], replicated
- new_var: float32 [3072], replicated
Inputs may be any that keep to these rules, and one draw needn't show every extreme that they name: `counts`: filled image slots of each batch group; at least one group is full in every draw.
All inputs are finite; a program needn't handle non-finite values.
Results may differ from a plain program's by a relative error of at most 0.019.
Values may be sent and summed in bfloat16 or wider, within the bound.
A program may use at most 192 MiB of HBM per device.

v0:
```python
import jax
import jax.numpy as jnp
from jax import lax
from jax.sharding import PartitionSpec as P

EPS = 1e-05
MOMENTUM = 0.1


def passed_along(block, axis, distance):
    devices = range(lax.axis_size(axis))
    route = [(i - distance, i) for i in devices if i - distance in devices]
    return lax.ppermute(block, axis, route)


def padded_2(block, sides, width):
    for axis, dim in sides:
        count = lax.axis_size(axis)
        forward = [(i, i + 1) for i in range(count - 1)]
        backward = [(target, source) for source, target in forward]
        low = lax.ppermute(
            lax.slice_in_dim(block, block.shape[dim] - width, None, axis=dim), axis, forward
        )
        high = lax.ppermute(lax.slice_in_dim(block, 0, width, axis=dim), axis, backward)
        block = jnp.concatenate([low, block, high], axis=dim)
    return block


def mish_act(values):
    return values * jnp.tanh(jax.nn.softplus(values))


def mish_back(before, grad_out):
    return jax.vjp(mish_act, before)[1](grad_out)[0]


def point_dot(left_op, right_op):
    return jnp.einsum("nhwc,cd->nhwd", left_op, right_op, preferred_element_type=jnp.float32)


def back_dot(left_op, right_op):
    return jnp.einsum("nhwd,cd->nhwc", left_op, right_op, preferred_element_type=jnp.float32)


def outer_dot(left_op, right_op):
    return jnp.einsum("nhwc,nhwd->cd", left_op, right_op, preferred_element_type=jnp.float32)


def norm_forward(values, valid_mask, gain_vec, offset, local_pixels):
    sum_first = jnp.sum(values * valid_mask, axis=(0, 1, 2))
    sum_second = jnp.sum(values * values * valid_mask, axis=(0, 1, 2))
    sum_first, sum_second, pixel_total = lax.psum(
        (sum_first, sum_second, local_pixels), ("rows", "batch")
    )
    batch_mean = sum_first / pixel_total
    batch_var = sum_second / pixel_total - batch_mean * batch_mean
    inv_std = lax.rsqrt(batch_var + EPS)
    normed = (values - batch_mean) * inv_std
    return (normed * gain_vec + offset, normed, inv_std, batch_mean, batch_var, pixel_total)


def norm_back(grad_out, normed, inv_std, gain_vec, valid_mask, pixel_total):
    bias_grad, gain_grad = lax.psum(
        (jnp.sum(grad_out, axis=(0, 1, 2)), jnp.sum(grad_out * normed, axis=(0, 1, 2))),
        ("rows", "batch"),
    )
    grad_in = (
        gain_vec
        * inv_std
        * (grad_out - valid_mask * (bias_grad + normed * gain_grad) / pixel_total)
    )
    return (grad_in, gain_grad, bias_grad)


def on_device(
    inputs,
    counts,
    down_weight,
    left_weight,
    right_weight,
    reduce_weight,
    spread_weight,
    norm_gains,
    norm_biases,
    running_mean,
    running_var,
    section_cotangent,
    block_cotangent,
):
    n_slots, row_in, col_in, in_width = inputs.shape
    row_out = row_in // 2
    col_out = col_in // 2
    section_width = down_weight.shape[3]
    branch_width = right_weight.shape[1]
    bounds = [
        0,
        section_width,
        section_width + branch_width,
        section_width + 2 * branch_width,
        section_width + 3 * branch_width,
        section_width + 4 * branch_width,
    ]
    valid_mask = (
        (jnp.arange(n_slots, dtype=jnp.int32) < counts[0])
        .astype(jnp.float32)
        .reshape(n_slots, 1, 1, 1)
    )
    local_pixels = jnp.sum(valid_mask) * float(row_out * col_out)

    def gain_at(bn_index):
        return norm_gains[bounds[bn_index] : bounds[bn_index + 1]]

    def norm_at(values, bn_index):
        return norm_forward(
            values,
            valid_mask,
            gain_at(bn_index),
            norm_biases[bounds[bn_index] : bounds[bn_index + 1]],
            local_pixels,
        )

    rim_row = passed_along(inputs[:, row_in - 1 :], "rows", 1)
    padded = jnp.pad(jnp.concatenate([rim_row, inputs], axis=1), ((0, 0), (0, 0), (1, 1), (0, 0)))
    taps = []
    first_out = jnp.zeros((n_slots, row_out, col_out, section_width), jnp.float32)
    for row_tap in range(3):
        for col_tap in range(3):
            window = padded[
                :, row_tap : row_tap + 2 * row_out : 2, col_tap : col_tap + 2 * col_out : 2, :
            ]
            taps.append(window)
            first_out = first_out + point_dot(window, down_weight[row_tap, col_tap])
    z_one, normed_one, inv_one, mean_one, var_one, pixel_total = norm_at(first_out, 0)
    act_one = mish_act(z_one).astype(jnp.bfloat16)
    z_left, normed_left, inv_left, mean_left, var_left, pixel_total = norm_at(
        point_dot(act_one, left_weight), 1
    )
    act_left = mish_act(z_left)
    z_right, normed_right, inv_right, mean_right, var_right, pixel_total = norm_at(
        point_dot(act_one, right_weight), 2
    )
    act_right = mish_act(z_right)
    right_low = act_right.astype(jnp.bfloat16)
    z_mid, normed_mid, inv_mid, mean_mid, var_mid, pixel_total = norm_at(
        point_dot(right_low, reduce_weight), 3
    )
    act_mid = mish_act(z_mid).astype(jnp.bfloat16)
    mid_halo = padded_2(act_mid, (("rows", 1),), 1)
    mid_pad = jnp.pad(mid_halo, ((0, 0), (0, 0), (1, 1), (0, 0)))
    fourth_out = jnp.zeros((n_slots, row_out, col_out, branch_width), jnp.float32)
    for row_tap in range(3):
        for col_tap in range(3):
            fourth_out = fourth_out + point_dot(
                mid_pad[:, row_tap : row_tap + row_out, col_tap : col_tap + col_out, :],
                spread_weight[row_tap, col_tap],
            )
    z_four, normed_four, inv_four, mean_four, var_four, pixel_total = norm_at(fourth_out, 4)
    act_four = mish_act(z_four)
    section_out = (valid_mask * jnp.concatenate([act_left, act_right], axis=3)).astype(jnp.bfloat16)
    block_out = (valid_mask * (act_right + act_four)).astype(jnp.bfloat16)
    section_grad = valid_mask * section_cotangent.astype(jnp.float32)
    block_grad = valid_mask * block_cotangent.astype(jnp.float32)
    grad_four, gain_four, bias_four = norm_back(
        mish_back(z_four, block_grad), normed_four, inv_four, gain_at(4), valid_mask, pixel_total
    )
    grad_four = grad_four.astype(jnp.bfloat16)
    grad_halo = padded_2(grad_four, (("rows", 1),), 1)
    grad_pad = jnp.pad(grad_halo, ((0, 0), (0, 0), (1, 1), (0, 0)))
    spread_taps = []
    mid_grad = jnp.zeros((n_slots, row_out, col_out, branch_width), jnp.float32)
    for row_tap in range(3):
        for col_tap in range(3):
            spread_taps.append(
                outer_dot(
                    mid_pad[:, row_tap : row_tap + row_out, col_tap : col_tap + col_out, :],
                    grad_four,
                )
            )
            mid_grad = mid_grad + back_dot(
                grad_pad[
                    :, 2 - row_tap : 2 - row_tap + row_out, 2 - col_tap : 2 - col_tap + col_out, :
                ],
                spread_weight[row_tap, col_tap],
            )
    spread_grad = jnp.stack(spread_taps).reshape(spread_weight.shape)
    grad_mid, gain_mid, bias_mid = norm_back(
        mish_back(z_mid, mid_grad), normed_mid, inv_mid, gain_at(3), valid_mask, pixel_total
    )
    grad_mid = grad_mid.astype(jnp.bfloat16)
    reduce_grad = outer_dot(right_low, grad_mid)
    right_total = section_grad[..., branch_width:] + block_grad + back_dot(grad_mid, reduce_weight)
    grad_right, gain_right, bias_right = norm_back(
        mish_back(z_right, right_total),
        normed_right,
        inv_right,
        gain_at(2),
        valid_mask,
        pixel_total,
    )
    grad_right = grad_right.astype(jnp.bfloat16)
    grad_left, gain_left, bias_left = norm_back(
        mish_back(z_left, section_grad[..., :branch_width]),
        normed_left,
        inv_left,
        gain_at(1),
        valid_mask,
        pixel_total,
    )
    grad_left = grad_left.astype(jnp.bfloat16)
    left_grad = outer_dot(act_one, grad_left)
    right_grad = outer_dot(act_one, grad_right)
    one_total = back_dot(grad_left, left_weight) + back_dot(grad_right, right_weight)
    grad_one, gain_one, bias_one = norm_back(
        mish_back(z_one, one_total), normed_one, inv_one, gain_at(0), valid_mask, pixel_total
    )
    grad_one = grad_one.astype(jnp.bfloat16)
    down_taps = []
    spread_back = jnp.zeros(padded.shape, jnp.float32)
    for row_tap in range(3):
        for col_tap in range(3):
            down_taps.append(outer_dot(taps[row_tap * 3 + col_tap], grad_one))
            spread_back = spread_back.at[
                :, row_tap : row_tap + 2 * row_out : 2, col_tap : col_tap + 2 * col_out : 2, :
            ].add(back_dot(grad_one, down_weight[row_tap, col_tap]))
    down_grad = jnp.stack(down_taps).reshape(down_weight.shape)
    back_rim = passed_along(
        spread_back[:, 0:1, 1 : col_in + 1].astype(jnp.bfloat16), "rows", -1
    ).astype(jnp.float32)
    input_grad = spread_back[:, 1:, 1 : col_in + 1]
    input_grad = input_grad.at[:, row_in - 1 :].add(back_rim)
    flat_grads = jnp.concatenate(
        [
            down_grad.reshape(-1),
            left_grad.reshape(-1),
            right_grad.reshape(-1),
            reduce_grad.reshape(-1),
            spread_grad.reshape(-1),
        ]
    )
    row_share = lax.psum_scatter(
        flat_grads.astype(jnp.bfloat16), "rows", scatter_dimension=0, tiled=True
    )
    weight_share = lax.psum_scatter(row_share, "batch", scatter_dimension=0, tiled=True).astype(
        jnp.float32
    )
    gain_grads = jnp.concatenate([gain_one, gain_left, gain_right, gain_mid, gain_four])
    bias_grads = jnp.concatenate([bias_one, bias_left, bias_right, bias_mid, bias_four])
    means_all = jnp.concatenate([mean_one, mean_left, mean_right, mean_mid, mean_four])
    vars_all = jnp.concatenate([var_one, var_left, var_right, var_mid, var_four])
    new_mean = (1.0 - MOMENTUM) * running_mean + MOMENTUM * means_all
    new_var = (1.0 - MOMENTUM) * running_var + MOMENTUM * vars_all * (
        pixel_total / (pixel_total - 1.0)
    )
    return (
        section_out,
        block_out,
        input_grad.astype(jnp.bfloat16),
        weight_share,
        gain_grads,
        bias_grads,
        new_mean,
        new_var,
    )


def solution(mesh):
    placed = (
        P("batch", "rows", None, None),
        P("batch"),
        P(),
        P(),
        P(),
        P(),
        P(),
        P(),
        P(),
        P(),
        P(),
        P("batch", "rows", None, None),
        P("batch", "rows", None, None),
    )
    return jax.shard_map(
        on_device,
        mesh=mesh,
        in_specs=placed,
        out_specs=(
            P("batch", "rows", None, None),
            P("batch", "rows", None, None),
            P("batch", "rows", None, None),
            P(("rows", "batch")),
            P(),
            P(),
            P(),
            P(),
        ),
        check_vma=False,
    )
```

profile of v0, /device:TPU:17, one launch (start us, length us, event | category | flops | bytes accessed | tf_op | source)
XLA Modules:
  0.0 933.4 jit_solution(10613996620360544966)
XLA Ops:
  8.3 3.8 collective-permute-start
  16.0 2.0 fusion.3
  20.8 5.2 slice.272
  25.9 5.0 slice.270
  30.9 5.0 slice.268
  36.0 5.1 slice.266
  41.1 5.0 slice.264
  46.1 5.0 slice.262
  51.1 1.7 fusion.70
  58.1 1.7 fusion.86
  64.9 2.8 multiply_reduce_fusion.1
  67.7 39.8 %all-reduce.12 = (f32[1024]{0:T(1024)S(1)}, f32[]{:T(128)}, f32[1024]{0:T(1024)S(1)}) all-reduce(f32[1024]{0:T(1024)S(1)} %get-tuple-element.53, f32[]{:T(128)S(6)} %mul.507, f32[1024]{0:T(1024)S(1)} %get-tuple-element.52), channel_id=1, replica_groups=mesh['rows'=8,'batch'=4] {'rows','batch'}, use_global_device_ids=true, to_apply=%region_1.2 | all-reduce | flops 2049 | bytes 16392 | tf_op jit(solution)/shard_map/psum | solution.py:52
  111.4 38.9 %all-reduce.11 = (f32[512]{0:T(512)S(1)}, f32[512]{0:T(512)S(1)}) all-reduce(f32[512]{0:T(512)S(1)} %get-tuple-element.63, f32[512]{0:T(512)S(1)} %get-tuple-element.62), channel_id=1, replica_groups=mesh['rows'=8,'batch'=4] {'rows','batch'}, use_global_device_ids=true, to_apply=%region_13.14 | all-reduce | flops 1024 | bytes 8192 | tf_op jit(solution)/shard_map/psum | solution.py:52
  151.6 2.3 fusion.287
  153.9 2.2 multiply_reduce_fusion.10
  156.2 41.1 %all-reduce.10 = (f32[512]{0:T(512)S(1)}, f32[512]{0:T(512)S(1)}) all-reduce(f32[512]{0:T(512)S(1)} %get-tuple-element.59, f32[512]{0:T(512)S(1)} %get-tuple-element.58), channel_id=1, replica_groups=mesh['rows'=8,'batch'=4] {'rows','batch'}, use_global_device_ids=true, to_apply=%region_17.18 | all-reduce | flops 1024 | bytes 8192 | tf_op jit(solution)/shard_map/psum | solution.py:52
  200.2 3.4 collective-permute-start.2
  203.6 2.4 collective-permute-start.1
  206.1 1.8 fusion.108
  212.1 1.9 multiply_reduce_fusion.8
  214.0 39.9 %all-reduce.9 = (f32[512]{0:T(512)S(1)}, f32[512]{0:T(512)S(1)}) all-reduce(f32[512]{0:T(512)} %get-tuple-element.57, f32[512]{0:T(512)} %get-tuple-element.56), channel_id=1, replica_groups=mesh['rows'=8,'batch'=4] {'rows','batch'}, use_global_device_ids=true, to_apply=%region_21.22 | all-reduce | flops 1024 | bytes 8192 | tf_op jit(solution)/shard_map/psum | solution.py:52
  253.9 2.0 fusion.264
  256.5 3.4 fusion.283
  259.8 41.5 %all-reduce.8 = (f32[512]{0:T(512)}, f32[512]{0:T(512)}) all-reduce(f32[512]{0:T(512)} %get-tuple-element.69, f32[512]{0:T(512)} %get-tuple-element.68), channel_id=1, replica_groups=mesh['rows'=8,'batch'=4] {'rows','batch'}, use_global_device_ids=true, to_apply=%region_29.31 | all-reduce | flops 1024 | bytes 8192 | tf_op jit(solution)/shard_map/psum | solution.py:63
  301.3 1.9 multiply_convert_fusion.3
  303.2 3.1 collective-permute-start.4
  306.4 2.4 collective-permute-start.3
  314.7 4.5 copy.171
  322.6 1.7 fusion.282
  324.4 37.9 %all-reduce.7 = (f32[512]{0:T(512)S(1)}, f32[512]{0:T(512)S(1)}, f32[512]{0:T(512)S(1)}, f32[512]{0:T(512)S(1)}) all-reduce(f32[512]{0:T(512)S(1)} %copy-done.76, f32[512]{0:T(512)S(1)} %copy-done.77, f32[512]{0:T(512)S(1)} %get-tuple-element.67, f32[512]{0:T(512)S(1)} %get-tuple-element.66), channel_id=1, replica_groups=mesh['rows'=8,'batch'=4] {'rows','batch'}, use_global_device_ids=true, to_apply=%region_9.10 | all-reduce | flops 2048 | bytes 16384 | tf_op jit(solution)/shard_map/psum | solution.py:52
  363.7 2.0 multiply_convert_fusion.2
  365.8 3.0 fusion.281
  370.5 50.1 %all-reduce.6 = (f32[512]{0:T(512)S(1)}, f32[512]{0:T(512)S(1)}, f32[512]{0:T(512)S(1)}, f32[512]{0:T(512)S(1)}) all-reduce(f32[512]{0:T(512)S(1)} %get-tuple-element.71, f32[512]{0:T(512)S(1)} %get-tuple-element.70, f32[512]{0:T(512)S(1)} %get-tuple-element.65, ...), channel_id=1, replica_groups=mesh['rows'=8,'batch'=4] {'rows','batch'}, use_global_device_ids=true, to_apply=%region_25.27 | all-reduce | flops 2048 | bytes 16384 | tf_op jit(solution)/shard_map/psum | solution.py:63
  420.6 2.3 multiply_convert_fusion.1
  428.8 2.6 fusion.280
  431.4 39.1 %all-reduce.5 = (f32[1024]{0:T(1024)S(1)}, f32[1024]{0:T(1024)S(1)}) all-reduce(f32[1024]{0:T(1024)S(1)} %get-tuple-element.55, f32[1024]{0:T(1024)S(1)} %get-tuple-element.54), channel_id=1, replica_groups=mesh['rows'=8,'batch'=4] {'rows','batch'}, use_global_device_ids=true, to_apply=%region_41.43 | all-reduce | flops 2048 | bytes 16384 | tf_op jit(solution)/shard_map/psum | solution.py:63
  470.5 3.1 multiply_convert_fusion
  486.7 9.7 %copy.167 = bf16[576,8,8,128]{3,1,2,0:T(8,128)(2,1)} copy(bf16[576,8,8,128]{3,2,1,0:T(8,128)(2,1)} %bitcast.219) | data formatting | bytes 18874368
  496.4 9.5 %constant_dynamic-update-slice_fusion = bf16[8388608]{0:T(1024)(128)(2,1)} fusion(bf16[4718592]{0:T(1024)(128)(2,1)} %bitcast.546), kind=kLoop, calls=%fused_computation.360 | loop fusion | bytes 18874368
  510.0 2.5 constant_dynamic-update-slice_fusion.21
  517.6 1.7 fusion.100
  520.4 2.0 fusion.96
  526.3 1.7 fusion.88
  528.4 1.8 fusion.84
  530.5 1.7 fusion.80
  532.5 1.7 fusion.76
  534.5 1.7 fusion.72
  536.6 1.7 fusion.68
  538.6 1.9 broadcast_in_dim.38
  540.5 5.3 scatter_fusion
  545.8 5.1 scatter_fusion.1
  550.9 5.0 scatter_fusion.2
  555.9 4.5 scatter_fusion.3
  560.4 4.6 scatter_fusion.4
  565.0 4.5 scatter_fusion.5
  569.6 4.6 scatter_fusion.6
  574.2 4.6 scatter_fusion.7
  578.7 4.6 scatter_fusion.8
  584.4 3.3 collective-permute-start.5
  587.8 263.0 %all-reduce.16.cloned.1.call-done = bf16[8388608]{0:T(1024)(128)(2,1)} async-done(((bf16[8388608]{0:T(1024)(128)(2,1)}), bf16[8388608]{0:T(1024)(128)(2,1)}) %all-reduce.16.cloned.1.call-update) | async-done | bytes 16777232
  850.8 3.2 dynamic-slice.9
  854.8 1.7 slice.360
  859.5 64.5 %all-reduce.18.cloned.1.call-done = bf16[1048576]{0:T(1024)(128)(2,1)} async-done(((bf16[1048576]{0:T(1024)(128)(2,1)}), bf16[1048576]{0:T(1024)(128)(2,1)}) %all-reduce.18.cloned.1.call-update) | async-done | bytes 2097168
  924.0 2.1 dynamic-slice_convert_fusion
  (333 shorter events, 78.3 us)
Async XLA Ops:
  7.2 103.0 %copy-start = (bf16[1024,512]{1,0:T(8,128)(2,1)S(1)}, bf16[1024,512]{1,0:T(8,128)(2,1)}, u32[]{:S(2)}) copy-start(bf16[1024,512]{1,0:T(8,128)(2,1)} %param.20) | copy-start | bytes 3145732
  7.2 843.6 %all-reduce.16.cloned.1.call-start = ((), (), s32[]{:S(2)}) async-start(), calls=%async_computation | async-start | bytes 33554432
  8.3 7.7 collective-permute-start
  12.7 141.2 %copy-start.48 = (f32[8]{0:T(128)}, f32[8]{0:T(128)S(1)}, u32[]{:S(2)}) copy-start(f32[8]{0:T(128)S(1)} %compare_convert_fusion) | copy-start | bytes 100
  14.0 95.4 %copy-start.66 = (f32[1024]{0:T(1024)}, f32[1024]{0:T(1024)S(1)}, u32[]{:S(2)}) copy-start(f32[1024]{0:T(1024)S(1)} %slice.281) | copy-start | bytes 12292
  16.0 135.6 %copy-start.78 = (f32[512]{0:T(512)}, f32[512]{0:T(512)S(1)}, u32[]{:S(2)}) copy-start(f32[512]{0:T(512)S(1)} %get-tuple-element.134) | copy-start | bytes 6148
  16.0 182.5 %copy-start.80 = (f32[512]{0:T(512)}, f32[512]{0:T(512)S(1)}, u32[]{:S(2)}) copy-start(f32[512]{0:T(512)S(1)} %get-tuple-element.136) | copy-start | bytes 6148
  19.2 37.0 %copy-start.9 = (bf16[8,2,16,512]{3,2,1,0:T(8,128)(2,1)}, bf16[8,2,16,512]{3,2,1,0:T(8,128)(2,1)S(1)}, u32[]{:S(2)}) copy-start(bf16[8,2,16,512]{3,2,1,0:T(8,128)(2,1)S(1)} %slice.278) | copy-start | bytes 786436
  20.0 36.3 %copy-start.11 = (bf16[8,2,16,512]{3,2,1,0:T(8,128)(2,1)}, bf16[8,2,16,512]{3,2,1,0:T(8,128)(2,1)S(1)}, u32[]{:S(2)}) copy-start(bf16[8,2,16,512]{3,2,1,0:T(8,128)(2,1)S(1)} %slice.276) | copy-start | bytes 786436
  20.8 35.5 %copy-start.13 = (bf16[8,2,16,512]{3,2,1,0:T(8,128)(2,1)}, bf16[8,2,16,512]{3,2,1,0:T(8,128)(2,1)S(1)}, u32[]{:S(2)}) copy-start(bf16[8,2,16,512]{3,2,1,0:T(8,128)(2,1)S(1)} %slice.274) | copy-start | bytes 786436
  51.1 6.9 copy-start.17
  52.8 7.0 copy-start.19
  54.5 6.9 copy-start.21
  56.3 6.9 copy-start.23
  58.0 6.8 copy-start.25
  58.0 6.8 copy-start.35
  64.9 44.0 %copy-start.63 = (f32[3072]{0:T(1024)S(1)}, f32[3072]{0:T(1024)}, u32[]{:S(2)}) copy-start(f32[3072]{0:T(1024)} %param.23) | copy-start | bytes 36868
  109.4 42.2 %copy-start.64 = (f32[1024]{0:T(1024)}, f32[1024]{0:T(1024)S(1)}, u32[]{:S(2)}) copy-start(f32[1024]{0:T(1024)S(1)} %get-tuple-element.129) | copy-start | bytes 12292
  109.4 100.1 %slice-start.2 = ((s8[4718592]{0:T(1024)(128)(4,1)}), s8[524288]{0:T(1024)(128)(4,1)S(1)}, s32[]{:S(2)}) async-start(s8[4718592]{0:T(1024)(128)(4,1)} %bitcast.550), calls=%async_computation.4 | async-start | bytes 1048576
  110.2 93.4 %copy-start.3 = (bf16[8,2,16,1024]{3,2,1,0:T(8,128)(2,1)}, bf16[8,2,16,1024]{3,2,1,0:T(8,128)(2,1)S(1)}, u32[]{:S(2)}) copy-start(bf16[8,2,16,1024]{3,2,1,0:T(8,128)(2,1)S(1)} %fusion.110) | copy-start | bytes 1572868
  151.6 45.7 %copy-start.72 = (f32[512]{0:T(512)}, f32[512]{0:T(512)S(1)}, u32[]{:S(2)}) copy-start(f32[512]{0:T(512)S(1)} %get-tuple-element.138) | copy-start | bytes 6148
  151.6 46.9 %copy-start.59 = (f32[512]{0:T(512)}, f32[512]{0:T(512)S(1)}, u32[]{:S(2)}) copy-start(f32[512]{0:T(512)S(1)} %get-tuple-element.102) | copy-start | bytes 6148
  151.6 48.6 %copy-start.52 = (f32[512]{0:T(512)}, f32[512]{0:T(512)S(1)}, u32[]{:S(2)}) copy-start(f32[512]{0:T(512)S(1)} %add_rsqrt_fusion.3) | copy-start | bytes 6148
  153.9 44.6 %copy-start.37 = (bf16[8,2,16,512]{3,2,1,0:T(8,128)(2,1)}, bf16[8,2,16,512]{3,2,1,0:T(8,128)(2,1)S(1)}, u32[]{:S(2)}) copy-start(bf16[8,2,16,512]{3,2,1,0:T(8,128)(2,1)S(1)} %get-tuple-element.112) | copy-start | bytes 786436
  198.5 11.4 %copy-start.46 = (f32[512]{0:T(512)}, f32[512]{0:T(512)S(1)}, u32[]{:S(2)}) copy-start(f32[512]{0:T(512)S(1)} %get-tuple-element.106) | copy-start | bytes 6148
  198.6 11.0 %slice-start.3 = ((s8[4718592]{0:T(1024)(128)(4,1)}), s8[4194304]{0:T(1024)(128)(4,1)S(1)}, s32[]{:S(2)}) async-start(s8[4718592]{0:T(1024)(128)(4,1)} %bitcast.550), calls=%async_computation.5 | async-start | bytes 8388608
  200.2 7.7 collective-permute-start.2
  203.6 4.3 collective-permute-start.1
  301.3 8.8 copy-start.31
  303.2 16.0 %collective-permute-start.4 = (bf16[8,1,16,512]{3,2,1,0:T(8,128)(2,1)S(1)}, bf16[8,1,16,512]{3,2,1,0:T(8,128)(2,1)S(1)}, u32[]{:S(2)}, u32[]{:S(2)}) collective-permute-start(bf16[8,1,16,512]{3,2,1,0:T(8,128)(2,1)S(1)} %get-tuple-element.125), channel_id=1, source_target_pairs={{4,0},{8,4},{12,8},{16,12},{20,16},{24,20},{28,24},{5,1},{9,5},{13... | collective-permute-start | bytes 393224 | tf_op jit(solution)/shard_map/ppermute | solution.py:24
  306.4 12.9 %collective-permute-start.3 = (bf16[8,1,16,512]{3,2,1,0:T(8,128)(2,1)S(1)}, bf16[8,1,16,512]{3,2,1,0:T(8,128)(2,1)S(1)}, u32[]{:S(2)}, u32[]{:S(2)}) collective-permute-start(bf16[8,1,16,512]{3,2,1,0:T(8,128)(2,1)S(1)} %get-tuple-element.124), channel_id=1, source_target_pairs={{0,4},{4,8},{8,12},{12,16},{16,20},{20,24},{24,28},{1,5},{5,9},{9,... | collective-permute-start | bytes 393224 | tf_op jit(solution)/shard_map/ppermute | solution.py:21
  321.8 40.5 %copy-start.51 = (f32[3072]{0:T(1024)S(1)}, f32[3072]{0:T(1024)}, u32[]{:S(2)}) copy-start(f32[3072]{0:T(1024)} %get-tuple-element.98) | copy-start | bytes 36868
  321.8 41.9 %copy-start.50 = (f32[8]{0:T(128)S(1)}, f32[8]{0:T(128)}, u32[]{:S(2)}) copy-start(f32[8]{0:T(128)} %copy-done.48) | copy-start | bytes 100
  321.8 41.9 %copy-start.82 = (f32[512]{0:T(512)S(1)}, f32[512]{0:T(512)}, u32[]{:S(2)}) copy-start(f32[512]{0:T(512)} %get-tuple-element.104) | copy-start | bytes 6148
  322.2 43.6 %copy-start.6 = (f32[8,2,16,512]{3,2,1,0:T(8,128)S(1)}, f32[8,2,16,512]{3,2,1,0:T(8,128)}, u32[]{:S(2)}) copy-start(f32[8,2,16,512]{3,2,1,0:T(8,128)} %get-tuple-element.156) | copy-start | bytes 1572868
  322.2 43.6 %copy-start.36 = (bf16[8,2,16,512]{3,2,1,0:T(8,128)(2,1)S(1)}, bf16[8,2,16,512]{3,2,1,0:T(8,128)(2,1)}, u32[]{:S(2)}) copy-start(bf16[8,2,16,512]{3,2,1,0:T(8,128)(2,1)} %param.28) | copy-start | bytes 786436
  322.2 43.6 %copy-start.53 = (f32[512]{0:T(512)S(1)}, f32[512]{0:T(512)}, u32[]{:S(2)}) copy-start(f32[512]{0:T(512)} %copy-done.52) | copy-start | bytes 6148
  322.2 43.6 %copy-start.73 = (f32[512]{0:T(512)S(1)}, f32[512]{0:T(512)}, u32[]{:S(2)}) copy-start(f32[512]{0:T(512)} %copy-done.72) | copy-start | bytes 6148
  322.2 43.6 %copy-start.79 = (f32[512]{0:T(512)S(1)}, f32[512]{0:T(512)}, u32[]{:S(2)}) copy-start(f32[512]{0:T(512)} %copy-done.78) | copy-start | bytes 6148
  324.3 44.5 %copy-start.85 = (f32[512]{0:T(512)S(1)}, f32[512]{0:T(512)}, u32[]{:S(2)}) copy-start(f32[512]{0:T(512)} %get-tuple-element.135) | copy-start | bytes 6148
  324.3 96.2 %copy-start.71 = (f32[512]{0:T(512)S(1)}, f32[512]{0:T(512)}, u32[]{:S(2)}) copy-start(f32[512]{0:T(512)} %get-tuple-element.101) | copy-start | bytes 6148
  368.8 55.8 %copy-start.4 = (bf16[8,2,16,1024]{3,2,1,0:T(8,128)(2,1)S(1)}, bf16[8,2,16,1024]{3,2,1,0:T(8,128)(2,1)}, u32[]{:S(2)}) copy-start(bf16[8,2,16,1024]{3,2,1,0:T(8,128)(2,1)} %copy-done.3) | copy-start | bytes 1572868
  428.8 41.7 %copy-start.2 = (f32[8,2,16,512]{3,2,1,0:T(8,128)S(1)}, f32[8,2,16,512]{3,2,1,0:T(8,128)}, u32[]{:S(2)}) copy-start(f32[8,2,16,512]{3,2,1,0:T(8,128)} %get-tuple-element.113) | copy-start | bytes 1572868
  428.8 41.7 %copy-start.8 = (f32[8,2,16,512]{3,2,1,0:T(8,128)S(1)}, f32[8,2,16,512]{3,2,1,0:T(8,128)}, u32[]{:S(2)}) copy-start(f32[8,2,16,512]{3,2,1,0:T(8,128)} %get-tuple-element.121) | copy-start | bytes 1572868
  428.8 41.7 %copy-start.68 = (f32[1024]{0:T(1024)S(1)}, f32[1024]{0:T(1024)}, u32[]{:S(2)}) copy-start(f32[1024]{0:T(1024)} %get-tuple-element.128) | copy-start | bytes 12292
  428.8 44.8 %copy-start.26 = (bf16[8,2,16,512]{3,2,1,0:T(8,128)(2,1)S(1)}, bf16[8,2,16,512]{3,2,1,0:T(8,128)(2,1)}, u32[]{:S(2)}) copy-start(bf16[8,2,16,512]{3,2,1,0:T(8,128)(2,1)} %slice.262) | copy-start | bytes 786436
  473.6 11.7 %copy-start.32 = (bf16[8,2,16,1024]{3,2,1,0:T(8,128)(2,1)}, bf16[8,2,16,1024]{3,2,1,0:T(8,128)(2,1)S(1)}, u32[]{:S(2)}) copy-start(bf16[8,2,16,1024]{3,2,1,0:T(8,128)(2,1)S(1)} %get-tuple-element.150) | copy-start | bytes 1572868
  496.4 13.6 %slice-start = ((s8[4718592]{0:T(1024)(128)(4,1)}), s8[4194304]{0:T(1024)(128)(4,1)S(1)}, s32[]{:S(2)}) async-start(s8[4718592]{0:T(1024)(128)(4,1)} %bitcast.547), calls=%async_computation.2 | async-start | bytes 8388608
  496.4 9.6 %copy-start.27 = (bf16[128,4,8,128]{3,2,1,0:T(8,128)(2,1)S(1)}, bf16[128,4,8,128]{3,2,1,0:T(8,128)(2,1)}, u32[]{:S(2)}) copy-start(bf16[128,4,8,128]{3,2,1,0:T(8,128)(2,1)} %fusion.23) | copy-start | bytes 3145732
  496.4 10.0 %copy-start.28 = (bf16[128,4,8,128]{3,2,1,0:T(8,128)(2,1)S(1)}, bf16[128,4,8,128]{3,2,1,0:T(8,128)(2,1)}, u32[]{:S(2)}) copy-start(bf16[128,4,8,128]{3,2,1,0:T(8,128)(2,1)} %fusion.24) | copy-start | bytes 3145732
  496.4 10.4 %copy-start.29 = (bf16[64,4,8,128]{3,2,1,0:T(8,128)(2,1)S(1)}, bf16[64,4,8,128]{3,2,1,0:T(8,128)(2,1)}, u32[]{:S(2)}) copy-start(bf16[64,4,8,128]{3,2,1,0:T(8,128)(2,1)} %fusion.60) | copy-start | bytes 1572868
  496.4 13.6 %slice-start.1 = ((s8[4718592]{0:T(1024)(128)(4,1)}), s8[524288]{0:T(1024)(128)(4,1)S(1)}, s32[]{:S(2)}) async-start(s8[4718592]{0:T(1024)(128)(4,1)} %bitcast.547), calls=%async_computation.3 | async-start | bytes 1048576
  512.6 411.5 %all-reduce.18.cloned.1.call-start = ((), (), s32[]{:S(2)}) async-start(), calls=%async_computation.1 | async-start | bytes 4194304
  574.1 279.9 %copy-start.60 = (f32[512]{0:T(512)S(1)}, f32[512]{0:T(512)}, u32[]{:S(2)}) copy-start(f32[512]{0:T(512)} %copy-done.59) | copy-start | bytes 6148
  574.1 280.0 %copy-start.62 = (f32[512]{0:T(512)S(1)}, f32[512]{0:T(512)}, u32[]{:S(2)}) copy-start(f32[512]{0:T(512)} %copy-done.61) | copy-start | bytes 6148
  574.1 280.0 %copy-start.74 = (f32[512]{0:T(512)S(1)}, f32[512]{0:T(512)}, u32[]{:S(2)}) copy-start(f32[512]{0:T(512)} %get-tuple-element.84) | copy-start | bytes 6148
  574.1 280.0 %copy-start.75 = (f32[512]{0:T(512)S(1)}, f32[512]{0:T(512)}, u32[]{:S(2)}) copy-start(f32[512]{0:T(512)} %get-tuple-element.85) | copy-start | bytes 6148
  574.1 280.0 %copy-start.69 = (f32[3072]{0:T(1024)S(1)}, f32[3072]{0:T(1024)}, u32[]{:S(2)}) copy-start(f32[3072]{0:T(1024)} %param.25) | copy-start | bytes 36868
  574.1 280.6 %copy-start.58 = (f32[512]{0:T(512)S(1)}, f32[512]{0:T(512)}, u32[]{:S(2)}) copy-start(f32[512]{0:T(512)} %copy-done.57) | copy-start | bytes 6148
  583.3 273.2 %copy-start.70 = (f32[3072]{0:T(1024)S(1)}, f32[3072]{0:T(1024)}, u32[]{:S(2)}) copy-start(f32[3072]{0:T(1024)} %param.26) | copy-start | bytes 36868
  584.4 272.7 %collective-permute-start.5 = (bf16[8,1,32,512]{3,0,2,1:T(8,128)(2,1)S(1)}, bf16[8,1,32,512]{3,0,2,1:T(8,128)(2,1)S(1)}, u32[]{:S(2)}, u32[]{:S(2)}) collective-permute-start(bf16[8,1,32,512]{3,0,2,1:T(8,128)(2,1)S(1)} %slice.546), channel_id=1, source_target_pairs={{4,0},{8,4},{12,8},{16,12},{20,16},{24,20},{28,24},{5,1},{9,5},{13... | collective-permute-start | bytes 786440 | tf_op jit(solution)/shard_map/ppermute | solution.py:13
  850.8 75.4 %copy-start.1 = (bf16[1024,512]{1,0:T(8,128)(2,1)S(1)}, bf16[1024,512]{1,0:T(8,128)(2,1)}, u32[]{:S(2)}) copy-start(bf16[1024,512]{1,0:T(8,128)(2,1)} %param.20) | copy-start | bytes 3145732
  854.2 72.0 %copy-start.86 = (f32[3072]{0:T(1024)}, f32[3072]{0:T(1024)S(1)}, u32[]{:S(2)}) copy-start(f32[3072]{0:T(1024)S(1)} %get-tuple-element.164) | copy-start | bytes 36868
  854.2 72.0 %copy-start.87 = (f32[3072]{0:T(1024)}, f32[3072]{0:T(1024)S(1)}, u32[]{:S(2)}) copy-start(f32[3072]{0:T(1024)S(1)} %get-tuple-element.165) | copy-start | bytes 36868
  (40 other events, 88.7 us)
Sparse Core Ops, SparseCore 0:
  512.7 338.0 all-reduce.15
  854.1 69.9 all-reduce.17
where the time goes:
time: 945 us; the launch traced here: 933 us
  waiting for transfers between devices  328 us (35%)
  blocking collectives  328 us (35%)
  local copies, waits for them, and re-layouts  86.9 us (9%)
  other arithmetic  77.6 us (8%)
  matrix products  74.2 us (8%)
  between operations  20.1 us (2%)
  starting transfers between devices  18.8 us (2%)
    unnamed x4, waiting for transfers between devices  328 us
    psum x5, blocking collectives, norm_forward(): lax.psum((sum_first, sum_second, local_pixels), ('rows', 'batch'))  198 us
    psum x3, blocking collectives, norm_back(): lax.psum((jnp.sum(grad_out, axis=(0, 1, 2)), jnp.sum(grad_out * normed, a...  131 us
    scatter-add x9, other arithmetic, on_device(): spread_back = spread_back.at[:, row_tap:row_tap + 2 * row_out:2, col_tap:...  42.8 us
    unnamed x218, local copies, waits for them, and re-layouts  36.3 us
    slice x9, local copies, waits for them, and re-layouts, on_device(): padded[:, row_tap:row_tap + 2 * row_out:2, col_tap:col_tap + 2 * col_out:...  33 us
    dot_general x21, matrix products, back_dot(): jnp.einsum('nhwd,cd->nhwc', left_op, right_op, preferred_element_type=jnp...  27.3 us
    dot_general x21, matrix products, point_dot(): jnp.einsum('nhwc,cd->nhwd', left_op, right_op, preferred_element_type=jnp...  26 us
  transfers between devices with their start and end apart: 8, of which 2 were waited for; matrix products, arithmetic and copies ran while one was open for 10% of the time, Pallas kernels for 0%

commit v1 on v0

--- a/solution.py
+++ b/solution.py
@@ -1,6 +1,11 @@
+import functools
+import types
+
 import jax
 import jax.numpy as jnp
 from jax import lax
+from jax.experimental import pallas as pl
+from jax.experimental.pallas import tpu as pltpu
 from jax.sharding import PartitionSpec as P
 
 EPS = 1e-05
@@ -263,6 +268,1077 @@
     )
 
 
+MESHID = pl.DeviceIdType.MESH
+BF = jnp.bfloat16
+F32 = jnp.float32
+NT = (((1,), (1,)), ((), ()))
+
+
+def mm(lhs, rhs):
+    return jnp.dot(lhs, rhs, preferred_element_type=F32)
+
+
+def mm_nt(lhs, rhs):
+    return lax.dot_general(lhs, rhs, NT, preferred_element_type=F32)
+
+
+def mish_parts(z):
+    e = jnp.exp(jnp.minimum(z, 20.0))
+    n = e * (e + 2.0)
+    d = 1.0 / (n + 2.0)
+    return e, d, n * d
+
+
+def mish_of(z):
+    return z * mish_parts(z)[2]
+
+
+def mish_slope(z):
+    e, d, t = mish_parts(z)
+    return t + 4.0 * z * (e * (1.0 + e)) * (d * d)
+
+
+def al(i, m):
+    return pl.multiple_of(i, m)
+
+
+def scratch_table():
+    v = pltpu.VMEM
+    dma = pltpu.SemaphoreType.DMA
+    table = dict(
+        inraw=v((5, 8, 32, 512), BF),
+        tmpc=v((8, 4, 40, 128), F32),
+        pad=v((8, 32, 512), F32),
+        X=v((2304, 512), BF),
+        xst=v((5, 512, 512), BF),
+        XG=v((3, 256, 2048), BF),
+        wd=v((9, 512, 1024), BF),
+        wl=v((1024, 512), BF),
+        wr=v((1024, 512), BF),
+        wm=v((512, 512), BF),
+        ws=v((9, 512, 512), BF),
+        sc=v((2, 8, 16, 1024), BF),
+        bc=v((4, 8, 16, 512), BF),
+        so=v((2, 8, 16, 1024), BF),
+        bo=v((2, 8, 16, 512), BF),
+        y1=v((256, 1024), F32),
+        d1=v((256, 1024), F32),
+        act1=v((256, 1024), BF),
+        yl=v((256, 512), F32),
+        yr=v((256, 512), F32),
+        gl=v((256, 512), F32),
+        dr=v((256, 512), F32),
+        actr=v((256, 512), F32),
+        rlow=v((256, 512), BF),
+        ym=v((512, 512), F32),
+        dm=v((256, 512), F32),
+        y4=v((512, 512), F32),
+        g4=v((512, 512), F32),
+        gm=v((256, 512), BF),
+        gr=v((256, 512), BF),
+        glb=v((256, 512), BF),
+        GA=v((512, 512), BF),
+        GB=v((512, 512), BF),
+        G4=v((512, 512), BF),
+        J2X=v((4, 512, 512), BF),
+        MT=v((4, 512, 512), BF),
+        st2=v((4, 512, 512), BF),
+        pr2=v((3, 512, 512), BF),
+        pr3=v((3, 512, 512), BF),
+        Gall=v((2048, 1024), BF),
+        G0=v((384, 1024), BF),
+        Gp=v((256 + 128, 1024), BF),
+        igf=v((2, 512, 128), F32),
+        zb=v((3, 4, 256, 256), BF),
+        za=v((3, 4, 256, 256), BF),
+        zs=v((4, 4, 256, 256), BF),
+        tile=v((256, 256), F32),
+        wgo=v((2048, 128), F32),
+        bn0=v((8, 1024), F32),
+        bnl=v((8, 512), F32),
+        bnr=v((8, 512), F32),
+        bnm=v((8, 512), F32),
+        bn4=v((8, 512), F32),
+        tot=v((1, 1024), F32),
+        ld=dma((32,)),
+        ldo=dma((16,)),
+        hs=dma((12,)),
+        hr=dma((12,)),
+        cs=dma((8,)),
+        cr=dma((8,)),
+        as_=dma((8,)),
+        ar_=dma((8,)),
+        xs=dma((3, 8)),
+        xr=dma((3, 8)),
+        bs=dma((12,)),
+        br=dma((12,)),
+        ps=dma((2, 4)),
+        pr=dma((2, 3)),
+        gs=dma((4, 3)),
+        grs=dma((4, 3)),
+        gfs=dma((4, 4)),
+        gfr=dma((4, 4)),
+        zus=dma((4, 4)),
+        zur=dma((4, 4)),
+        zds=dma((4, 4)),
+        zdr=dma((4, 4)),
+    )
+    widths = AR_WIDTHS
+    for k, w in enumerate(widths):
+        table["ar_st%d" % k] = v((2, w), F32)
+        table["ar_ct%d" % k] = v((2, w), F32)
+        table["ar_ab%d" % k] = v((16, 2, w), F32)
+    return table
+
+
+AR_WIDTHS = (1152, 1024, 512, 512, 1024, 512, 512, 1024)
+
+
+def fused_kernel(names, n_in, n_out, *refs):
+    (in_ref, cnt_ref, wd_ref, wl_ref, wr_ref, wm_ref, ws_ref, gain_ref, bias_ref, rm_ref, rv_ref,
+     sc_ref, bc_ref) = refs[:n_in]
+    (so_ref, bo_ref, ig_ref, wg_ref, gg_ref, bg_ref, nm_ref, nv_ref) = refs[n_in : n_in + n_out]
+    s = types.SimpleNamespace(**dict(zip(names, refs[n_in + n_out :])))
+    st = [getattr(s, "ar_st%d" % k) for k in range(8)]
+    ct = [getattr(s, "ar_ct%d" % k) for k in range(8)]
+    ab = [getattr(s, "ar_ab%d" % k) for k in range(8)]
+
+    r = lax.axis_index("rows")
+    b = lax.axis_index("batch")
+    z = r // 2
+    c = r % 2
+    y = b // 2
+    x = b % 2
+    chip = z * 4 + b
+    sib = (r + 1 - 2 * c, b)
+    own8 = c * 4 + b
+    first = r == 0
+    last = r == 7
+
+    def remote(src, dst, ss, rs, dev):
+        return pltpu.make_async_remote_copy(
+            src_ref=src, dst_ref=dst, send_sem=ss, recv_sem=rs, device_id=dev, device_id_type=MESHID
+        )
+
+    def recv_wait(dst, rs):
+        pltpu.make_async_copy(dst, dst, rs).wait()
+
+    bar = pltpu.get_barrier_semaphore()
+    for i in range(8):
+        for j in range(4):
+            if i or j:
+                pl.semaphore_signal(
+                    bar, inc=1, device_id=((r + i) % 8, (b + j) % 4), device_id_type=MESHID
+                )
+
+    loads = {}
+
+    def load(name, src, dst):
+        cp = pltpu.make_async_copy(src, dst, s.ld.at[len(loads)])
+        cp.start()
+        loads[name] = cp
+
+    for i in range(4):
+        load("in%d" % i, in_ref.at[:, i], s.inraw.at[1 + i])
+    for t in (3, 4, 5, 6, 7, 8, 0, 1, 2):
+        load("wd%d" % t, wd_ref.at[t], s.wd.at[t])
+    load("wl", wl_ref, s.wl)
+    load("wr", wr_ref, s.wr)
+    load("wm", wm_ref, s.wm)
+    for i in range(2):
+        load("sc%d" % i, sc_ref.at[:, i], s.sc.at[i])
+        load("bc%d" % i, bc_ref.at[:, i], s.bc.at[1 + i])
+    for i in range(3):
+        load("ws%d" % i, ws_ref.at[pl.ds(3 * i, 3)], s.ws.at[pl.ds(3 * i, 3)])
+
+    for n in range(8):
+        for q in range(4):
+            s.tmpc[n, q, 0:8, :] = jnp.zeros((8, 128), F32)
+        s.pad[n, 0:8, :] = jnp.zeros((8, 512), F32)
+        s.pad[n, 24:32, :] = jnp.zeros((8, 512), F32)
+
+    @pl.when(first)
+    def _():
+        s.inraw[0] = jnp.zeros((8, 32, 512), BF)
+        s.bc[0] = jnp.zeros((8, 16, 512), BF)
+        s.ym[0:128, :] = jnp.zeros((128, 512), F32)
+        s.y4[0:128, :] = jnp.zeros((128, 512), F32)
+
+    @pl.when(last)
+    def _():
+        s.bc[3] = jnp.zeros((8, 16, 512), BF)
+        s.ym[384:512, :] = jnp.zeros((128, 512), F32)
+        s.y4[384:512, :] = jnp.zeros((128, 512), F32)
+        s.G0[256:384, :] = jnp.zeros((128, 1024), BF)
+
+    pl.semaphore_wait(bar, 31)
+
+    nxt = (r + 1, b)
+    prv = (r - 1, b)
+
+    def halo_down(k, src, dst):
+        @pl.when(r < 7)
+        def _():
+            remote(src, dst, s.hs.at[k], s.hr.at[k], nxt).start()
+
+    def halo_up(k, src, dst):
+        @pl.when(r > 0)
+        def _():
+            remote(src, dst, s.hs.at[k], s.hr.at[k], prv).start()
+
+    def halo_down_wait(k, dst):
+        @pl.when(r < 7)
+        def _():
+            pltpu.make_async_copy(dst, dst, s.hs.at[k]).wait()
+
+        @pl.when(r > 0)
+        def _():
+            recv_wait(dst, s.hr.at[k])
+
+    def halo_up_wait(k, dst):
+        @pl.when(r > 0)
+        def _():
+            pltpu.make_async_copy(dst, dst, s.hs.at[k]).wait()
+
+        @pl.when(r < 7)
+        def _():
+            recv_wait(dst, s.hr.at[k])
+
+    halo_down(0, in_ref.at[:, 3], s.inraw.at[0])
+    halo_down(1, bc_ref.at[:, 1], s.bc.at[0])
+    halo_up(2, bc_ref.at[:, 0], s.bc.at[3])
+
+    count = cnt_ref[0]
+    vs = [(jnp.int32(n) < count).astype(F32) for n in range(8)]
+
+    def ar_send(k):
+        cp = remote(st[k], ct[k], s.cs.at[k], s.cr.at[k], sib)
+        cp.start()
+        cp.wait()
+        ab[k][chip] = st[k][...] + ct[k][...]
+        for j in range(1, 16):
+            dev = (((z + j // 4) % 4) * 2 + c, (b + j % 4) % 4)
+            remote(ab[k].at[chip], ab[k].at[chip], s.as_.at[k], s.ar_.at[k], dev).start()
+
+    def ar_recv(k):
+        part = ab[k].at[pl.ds(0, 15)]
+        pltpu.make_async_copy(part, part, s.ar_.at[k]).wait()
+        pltpu.make_async_copy(part, part, s.as_.at[k]).wait()
+        out = ab[k][0]
+        for j in range(1, 16):
+            out = out + ab[k][j]
+        return out
+
+    def colstats(acc, k, col, width):
+        a = acc.reshape(2, 8, 16, width)
+        t1 = jnp.zeros((16, width), F32)
+        t2 = jnp.zeros((16, width), F32)
+        for n in range(8):
+            p = a[0, n]
+            q = a[1, n]
+            t1 = t1 + (p + q) * vs[n]
+            t2 = t2 + (p * p + q * q) * vs[n]
+        st[k][0:1, pl.ds(col, width)] = jnp.sum(t1, axis=0, keepdims=True)
+        st[k][1:2, pl.ds(col, width)] = jnp.sum(t2, axis=0, keepdims=True)
+
+    def tiles(count_, body, init=0, unroll=2):
+        return lax.fori_loop(0, count_, body, init, unroll=unroll)
+
+    def rows16(i):
+        return pl.ds(al(i * 16, 16), 16)
+
+    def deinterleave(slot):
+        targets = [(i, rr) for rr in range(2) for i in range(3) if i + 2 * rr == slot]
+
+        def body(n, _):
+            for q in range(4):
+                s.tmpc[n, q, 8:40, :] = s.inraw[slot, n, :, q * 128 : q * 128 + 128].astype(F32)
+            for j in range(3):
+                for q in range(4):
+                    val = s.tmpc[n, q, pl.ds(7 + j, 16, stride=2), :].astype(BF)
+                    for i, rr in targets:
+                        s.X[pl.ds(al((3 * i + j) * 256 + rr * 128 + n * 16, 16), 16), q * 128 : q * 128 + 128] = val
+            return 0
+
+        lax.fori_loop(0, 8, body, 0)
+
+    for i in range(4):
+        loads["in%d" % i].wait()
+        deinterleave(1 + i)
+    for t in (3, 4, 5, 6, 7, 8):
+        loads["wd%d" % t].wait()
+
+    def conv_a(n, _):
+        cols = pl.ds(al(n * 256, 256), 256)
+        acc = mm(s.X[3 * 256 : 4 * 256, :], s.wd[3, :, cols])
+        for t in range(4, 9):
+            acc = acc + mm(s.X[t * 256 : t * 256 + 256, :], s.wd[t, :, cols])
+        s.y1[:, cols] = acc
+        return 0
+
+    lax.fori_loop(0, 4, conv_a, 0)
+    halo_down_wait(0, s.inraw.at[0])
+    deinterleave(0)
+    for t in (0, 1, 2):
+        loads["wd%d" % t].wait()
+    st[0][:, 1024:1152] = jnp.zeros((2, 128), F32) + count.astype(F32) * 32.0
+
+    def conv_b(n, _):
+        col = al(n * 256, 256)
+        cols = pl.ds(col, 256)
+        acc = s.y1[:, cols]
+        for t in range(3):
+            acc = acc + mm(s.X[t * 256 : t * 256 + 256, :], s.wd[t, :, cols])
+        s.y1[:, cols] = acc
+        colstats(acc, 0, col, 256)
+        return 0
+
+    lax.fori_loop(0, 4, conv_b, 0)
+    ar_send(0)
+
+    def xpose(t, _):
+        for q in range(4):
+            s.xst[t // 2, q * 128 : q * 128 + 128, pl.ds(al((t % 2) * 256, 256), 256)] = s.X[
+                pl.ds(al(t * 256, 256), 256), q * 128 : q * 128 + 128
+            ].T
+        return 0
+
+    lax.fori_loop(0, 9, xpose, 0)
+
+    def x_send(dc, db, do):
+        cc = (c + dc) % 2
+        bb = (b + db) % 4
+        yy = bb // 2
+        xx = bb % 2
+        idx = dc * 4 + db
+        half = pl.ds(al(xx * 256, 256), 256)
+        mine = pl.ds(al(own8 * 256, 256), 256)
+        for k in range(3):
+            tap = 2 * cc + yy + 4 * k if k < 2 else 8
+
+            def go():
+                src = s.xst.at[tap // 2, half, pl.ds(al((tap % 2) * 256, 256), 256)]
+                dst = s.XG.at[k, :, mine]
+                if dc == 0 and db == 0:
+                    cp = pltpu.make_async_copy(src, dst, s.xs.at[k, idx])
+                else:
+                    cp = remote(src, dst, s.xs.at[k, idx], s.xr.at[k, idx], ((z * 2 + cc), bb))
+                do(cp)
+
+            if k == 2:
+                pl.when(jnp.logical_and(cc == 0, yy == 0))(go)
+            else:
+                go()
+
+    for dc in range(2):
+        for db in range(4):
+            x_send(dc, db, lambda cp: cp.start())
+
+    def norm_params(k, res, lo, bn, width):
+        g = gain_ref[0:1, pl.ds(lo, width)]
+        o = bias_ref[0:1, pl.ds(lo, width)]
+        inv_t = s.tot[0:1, 0:width]
+        mean = res[0:1] * inv_t
+        var = res[1:2] * inv_t - mean * mean
+        inv = lax.rsqrt(var + EPS)
+        a = g * inv
+        bn[0:1, :] = a
+        bn[1:2, :] = o - mean * a
+        bn[2:3, :] = inv
+        bn[3:4, :] = -mean * inv
+        nm_ref[0:1, pl.ds(lo, width)] = (1.0 - MOMENTUM) * rm_ref[0:1, pl.ds(lo, width)] + MOMENTUM * mean
+        t = 1.0 / inv_t
+        nv_ref[0:1, pl.ds(lo, width)] = (1.0 - MOMENTUM) * rv_ref[0:1, pl.ds(lo, width)] + MOMENTUM * var * (
+            t / (t - 1.0)
+        )
+
+    res = ar_recv(0)
+    s.tot[0:1, :] = jnp.broadcast_to(1.0 / res[0:1, 1024:1025], (1, 1024))
+    norm_params(0, res[:, 0:1024], 0, s.bn0, 1024)
+
+    def act_one(i, _):
+        zv = s.y1[rows16(i), :] * s.bn0[0:1, :] + s.bn0[1:2, :]
+        s.act1[rows16(i), :] = mish_of(zv).astype(BF)
+        return 0
+
+    tiles(16, act_one)
+    loads["wl"].wait()
+    loads["wr"].wait()
+
+    for h in range(2):
+        cols = pl.ds(h * 256, 256)
+        acc = mm(s.act1[...], s.wl[:, cols])
+        s.yl[:, cols] = acc
+        colstats(acc, 1, h * 256, 256)
+        acc = mm(s.act1[...], s.wr[:, cols])
+        s.yr[:, cols] = acc
+        colstats(acc, 1, 512 + h * 256, 256)
+    ar_send(1)
+
+    def slope_one(i, _):
+        zv = s.y1[rows16(i), :] * s.bn0[0:1, :] + s.bn0[1:2, :]
+        s.d1[rows16(i), :] = mish_slope(zv)
+        return 0
+
+    tiles(16, slope_one)
+    mycols = pl.ds(al(c * 256, 256), 256)
+
+    def xpose_act(h, _):
+        for q in range(4):
+            blk = s.act1[:, pl.ds(al(h * 512 + q * 128, 128), 128)]
+            s.J2X[2 - 2 * c + h, pl.ds(q * 128, 128), mycols] = blk.T
+        return 0
+
+    lax.fori_loop(0, 2, xpose_act, 0)
+    pair = []
+
+    def to_sib(src, dst):
+        k = len(pair)
+        cp = remote(src, dst, s.bs.at[k], s.br.at[k], sib)
+        pair.append(cp)
+        return cp
+
+    cp_act = to_sib(s.J2X.at[pl.ds(2 - 2 * c, 2), :, mycols], s.J2X.at[pl.ds(2 * c, 2), :, mycols])
+    cp_act.start()
+
+    res = ar_recv(1)
+    norm_params(1, res[:, 0:512], 1024, s.bnl, 512)
+    norm_params(2, res[:, 512:1024], 1536, s.bnr, 512)
+
+    def act_right(i, _):
+        zv = s.yr[rows16(i), :] * s.bnr[0:1, :] + s.bnr[1:2, :]
+        e, d, t = mish_parts(zv)
+        a = zv * t
+        s.actr[rows16(i), :] = a
+        s.rlow[rows16(i), :] = a.astype(BF)
+        s.dr[rows16(i), :] = t + 4.0 * zv * (e * (1.0 + e)) * (d * d)
+        return 0
+
+    tiles(16, act_right)
+    loads["wm"].wait()
+    for h in range(2):
+        cols = pl.ds(h * 256, 256)
+        acc = mm(s.rlow[...], s.wm[:, cols])
+        s.ym[128:384, cols] = acc
+        colstats(acc, 2, h * 256, 256)
+    ar_send(2)
+    halo_down(3, s.ym.at[pl.ds(256, 128)], s.ym.at[pl.ds(0, 128)])
+    halo_up(4, s.ym.at[pl.ds(128, 128)], s.ym.at[pl.ds(384, 128)])
+
+    loads["sc0"].wait()
+    loads["sc1"].wait()
+
+    def valid_at(i):
+        return ((i % 8) < count).astype(F32)
+
+    def left_branch(i, carry):
+        t1, t2 = carry
+        v = valid_at(i)
+        yv = s.yl[rows16(i), :]
+        zv = yv * s.bnl[0:1, :] + s.bnl[1:2, :]
+        e, d, t = mish_parts(zv)
+        s.so[i // 8, i % 8, :, 0:512] = (zv * t * v).astype(BF)
+        s.so[i // 8, i % 8, :, 512:1024] = (s.actr[rows16(i), :] * v).astype(BF)
+        gz = (t + 4.0 * zv * (e * (1.0 + e)) * (d * d)) * (s.sc[i // 8, i % 8, :, 0:512].astype(F32) * v)
+        s.gl[rows16(i), :] = gz
+        gx = gz * (yv * s.bnl[2:3, :] + s.bnl[3:4, :])
+        return t1 + gz, t2 + gx
+
+    zero16 = jnp.zeros((16, 512), F32)
+    t1, t2 = tiles(16, left_branch, (zero16, zero16), unroll=1)
+    st[4][0:1, 512:1024] = jnp.sum(t1, axis=0, keepdims=True)
+    st[4][1:2, 512:1024] = jnp.sum(t2, axis=0, keepdims=True)
+    outs = []
+
+    def store(src, dst):
+        cp = pltpu.make_async_copy(src, dst, s.ldo.at[len(outs)])
+        cp.start()
+        outs.append(cp)
+
+    for i in range(2):
+        store(s.so.at[i], so_ref.at[:, i])
+    for q in range(4):
+        s.J2X[2 * c, pl.ds(q * 128, 128), mycols] = s.rlow[:, q * 128 : q * 128 + 128].T
+    cp_low = to_sib(s.J2X.at[0, :, mycols], s.J2X.at[2, :, mycols])
+
+    @pl.when(c == 0)
+    def _():
+        cp_low.start()
+
+    res = ar_recv(2)
+    norm_params(3, res, 2048, s.bnm, 512)
+    halo_down_wait(3, s.ym.at[pl.ds(0, 128)])
+    halo_up_wait(4, s.ym.at[pl.ds(384, 128)])
+
+    def edge_at(i):
+        lo = jnp.logical_and(i < 8, first)
+        hi = jnp.logical_and(i >= 24, last)
+        return 1.0 - jnp.logical_or(lo, hi).astype(F32)
+
+    def windows(i, val):
+        n = i % 8
+        s.pad[n, 8:24, :] = val
+        for k in range(3):
+            rows = pl.ds(al(k * 512 + i * 16, 16), 16)
+            s.X[rows, :] = (val if k == 1 else s.pad[n, 7 + k : 23 + k, :]).astype(BF)
+
+    def act_mid(i, _):
+        zv = s.ym[rows16(i), :] * s.bnm[0:1, :] + s.bnm[1:2, :]
+        windows(i, mish_of(zv) * edge_at(i))
+        return 0
+
+    tiles(32, act_mid)
+    for i in range(3):
+        loads["ws%d" % i].wait()
+
+    def conv_four(h, _):
+        col = al(h * 256, 256)
+        cols = pl.ds(col, 256)
+        acc = None
+        for t in range(9):
+            part = mm(s.X[pl.ds((t % 3) * 512 + (t // 3) * 128, 256), :], s.ws[t, :, cols])
+            acc = part if acc is None else acc + part
+        s.y4[pl.ds(128, 256), cols] = acc
+        colstats(acc, 3, col, 256)
+        return 0
+
+    lax.fori_loop(0, 2, conv_four, 0)
+    ar_send(3)
+    halo_down(5, s.y4.at[pl.ds(256, 128)], s.y4.at[pl.ds(0, 128)])
+    halo_up(6, s.y4.at[pl.ds(128, 128)], s.y4.at[pl.ds(384, 128)])
+
+    def slope_mid(i, _):
+        zv = s.ym[pl.ds(al(128 + i * 16, 16), 16), :] * s.bnm[0:1, :] + s.bnm[1:2, :]
+        s.dm[rows16(i), :] = mish_slope(zv)
+        return 0
+
+    tiles(16, slope_mid)
+
+    def window_t(tap, dst, k):
+        base = pl.ds(al((tap % 3) * 512 + (tap // 3) * 128, 128), 256)
+        for q in range(4):
+            dst[k, pl.ds(q * 128, 128), mycols] = s.X[base, q * 128 : q * 128 + 128].T
+
+    def xpose_mid(k, _):
+        window_t(1 + 4 * c + k, s.MT, k)
+        window_t(5 - 4 * c + k, s.st2, k)
+        return 0
+
+    lax.fori_loop(0, 4, xpose_mid, 0)
+    window_t(0 * c, s.J2X, 1 + 2 * c)
+    cp_mt = to_sib(s.st2.at[:, :, mycols], s.MT.at[:, :, mycols])
+    cp_mt.start()
+    cp_m0 = to_sib(s.J2X.at[1, :, mycols], s.J2X.at[3, :, mycols])
+
+    @pl.when(c == 0)
+    def _():
+        cp_m0.start()
+
+    loads["bc0"].wait()
+    loads["bc1"].wait()
+    halo_down_wait(1, s.bc.at[0])
+    halo_up_wait(2, s.bc.at[3])
+
+    res = ar_recv(3)
+    norm_params(4, res, 2560, s.bn4, 512)
+
+    def norm_four(i, carry):
+        t1, t2 = carry
+        v = valid_at(i)
+        rows = pl.ds(al(128 + i * 16, 16), 16)
+        yv = s.y4[rows, :]
+        zv = yv * s.bn4[0:1, :] + s.bn4[1:2, :]
+        e, d, t = mish_parts(zv)
+        s.bo[i // 8, i % 8] = ((zv * t + s.actr[rows16(i), :]) * v).astype(BF)
+        gz = (t + 4.0 * zv * (e * (1.0 + e)) * (d * d)) * (s.bc[1 + i // 8, i % 8].astype(F32) * v)
+        s.g4[rows, :] = gz
+        gx = gz * (yv * s.bn4[2:3, :] + s.bn4[3:4, :])
+        return t1 + gz, t2 + gx
+
+    t1, t2 = tiles(16, norm_four, (zero16, zero16), unroll=1)
+    st[4][0:1, 0:512] = jnp.sum(t1, axis=0, keepdims=True)
+    st[4][1:2, 0:512] = jnp.sum(t2, axis=0, keepdims=True)
+    ar_send(4)
+    for i in range(2):
+        store(s.bo.at[i], bo_ref.at[:, i])
+
+    halo_down_wait(5, s.y4.at[pl.ds(0, 128)])
+    halo_up_wait(6, s.y4.at[pl.ds(384, 128)])
+
+    def halo_four(k, _):
+        i = k + 16 * (k // 8)
+        v = valid_at(i)
+        zv = s.y4[rows16(i), :] * s.bn4[0:1, :] + s.bn4[1:2, :]
+        s.g4[rows16(i), :] = mish_slope(zv) * (s.bc[i // 8, i % 8].astype(F32) * v)
+        return 0
+
+    tiles(16, halo_four)
+
+    def back_params(res, lo, bn, width):
+        inv_t = s.tot[0:1, 0:width]
+        bg_ref[0:1, pl.ds(lo, width)] = res[0:1]
+        gg_ref[0:1, pl.ds(lo, width)] = res[1:2]
+        bn[4:5, :] = res[0:1] * inv_t
+        bn[5:6, :] = res[1:2] * inv_t
+
+    def grad_of(gz, yv, bn, v):
+        xh = yv * bn[2:3, :] + bn[3:4, :]
+        return bn[0:1, :] * (gz - v * (bn[4:5, :] + xh * bn[5:6, :]))
+
+    res = ar_recv(4)
+    back_params(res[:, 0:512], 2560, s.bn4, 512)
+    back_params(res[:, 512:1024], 1024, s.bnl, 512)
+
+    def grad_four(i, _):
+        v = valid_at(i) * edge_at(i)
+        windows(i, grad_of(s.g4[rows16(i), :], s.y4[rows16(i), :], s.bn4, v).astype(BF).astype(F32))
+        return 0
+
+    tiles(32, grad_four)
+
+    def back_four(h, _):
+        col = al(h * 256, 256)
+        acc = None
+        for t in range(9):
+            part = mm_nt(
+                s.X[pl.ds((2 - t % 3) * 512 + (2 - t // 3) * 128, 256), :], s.ws[t, pl.ds(col, 256), :]
+            )
+            acc = part if acc is None else acc + part
+        cols = pl.ds(col, 256)
+        gz = s.dm[:, cols] * acc
+        s.dm[:, cols] = gz
+        xh = s.ym[pl.ds(128, 256), cols] * s.bnm[2:3, cols] + s.bnm[3:4, cols]
+        st[5][0:1, cols] = jnp.sum(gz, axis=0, keepdims=True)
+        st[5][1:2, cols] = jnp.sum(gz * xh, axis=0, keepdims=True)
+        return 0
+
+    lax.fori_loop(0, 2, back_four, 0)
+    ar_send(5)
+
+    def grad_left(i, _):
+        val = grad_of(s.gl[rows16(i), :], s.yl[rows16(i), :], s.bnl, valid_at(i)).astype(BF)
+        s.glb[rows16(i), :] = val
+        s.GA[pl.ds(al(c * 256 + i * 16, 16), 16), :] = val
+        return 0
+
+    tiles(16, grad_left)
+    myrows = pl.ds(al(c * 256, 256), 256)
+    s.G4[myrows, :] = s.X[640:896, :]
+    cp_g4 = to_sib(s.G4.at[myrows], s.G4.at[myrows])
+    cp_g4.start()
+    cp_ga = to_sib(s.glb, s.GA.at[myrows])
+
+    @pl.when(c == 1)
+    def _():
+        cp_ga.start()
+
+    def both_waits(cp, sender):
+        pl.when(c == sender)(cp.wait_send)
+        pl.when(c != sender)(cp.wait_recv)
+
+    cp_act.wait()
+    both_waits(cp_low, 0)
+    cp_mt.wait()
+    both_waits(cp_m0, 0)
+    cp_g4.wait()
+
+    def plane_send(job, stage, k, slots):
+        rel = (k - b + 4) % 4
+
+        @pl.when(rel > 0)
+        def _():
+            remote(
+                stage.at[k], slots.at[rel - 1], s.ps.at[job, k], s.pr.at[job, rel - 1], (r, k)
+            ).start()
+
+    def piece(lhs, k, rhs, stage):
+        def body(i, _):
+            rows = pl.ds(al((i // 2) * 256, 256), 256)
+            cols = pl.ds(al((i % 2) * 256, 256), 256)
+            stage[k, rows, cols] = mm(lhs[k, rows, :], rhs[:, cols]).astype(BF)
+            return 0
+
+        lax.fori_loop(0, 4, body, 0)
+
+    for dc in range(2):
+        for db in range(4):
+            x_wait = lambda cp, me=(dc == 0 and db == 0): cp.wait() if me else cp.wait_send()
+            x_send(dc, db, x_wait)
+    st3 = s.xst
+    for k in range(4):
+        piece(s.MT, k, s.G4, st3)
+        plane_send(0, st3, k, s.pr3)
+
+    both_waits(cp_ga, 1)
+
+    @pl.when(c == 0)
+    def _():
+        for k in (2, 3):
+            piece(s.J2X, k, s.GA, s.st2)
+            plane_send(1, s.st2, k, s.pr2)
+
+    @pl.when(c == 1)
+    def _():
+        piece(s.J2X, 3, s.G4, s.st2)
+        plane_send(1, s.st2, 3, s.pr2)
+
+    res = ar_recv(5)
+    back_params(res, 2048, s.bnm, 512)
+
+    def grad_mid(i, _):
+        val = grad_of(
+            s.dm[rows16(i), :], s.ym[pl.ds(al(128 + i * 16, 16), 16), :], s.bnm, valid_at(i)
+        ).astype(BF)
+        s.gm[rows16(i), :] = val
+        s.GB[pl.ds(al(c * 256 + i * 16, 16), 16), :] = val
+        return 0
+
+    tiles(16, grad_mid)
+
+    def back_mid(h, _):
+        col = al(h * 256, 256)
+        cols = pl.ds(col, 256)
+        acc = mm_nt(s.gm[...], s.wm[cols, :]).reshape(2, 8, 16, 256)
+        t1 = jnp.zeros((16, 256), F32)
+        t2 = jnp.zeros((16, 256), F32)
+        for rr in range(2):
+            for n in range(8):
+                rows = pl.ds(rr * 128 + n * 16, 16)
+                cot = s.sc[rr, n, :, pl.ds(al(512 + h * 256, 256), 256)].astype(F32) + s.bc[
+                    1 + rr, n, :, cols
+                ].astype(F32)
+                gz = s.dr[rows, cols] * (acc[rr, n] + cot * vs[n])
+                s.dr[rows, cols] = gz
+                t1 = t1 + gz
+                t2 = t2 + gz * (s.yr[rows, cols] * s.bnr[2:3, cols] + s.bnr[3:4, cols])
+        st[6][0:1, cols] = jnp.sum(t1, axis=0, keepdims=True)
+        st[6][1:2, cols] = jnp.sum(t2, axis=0, keepdims=True)
+        return 0
+
+    lax.fori_loop(0, 2, back_mid, 0)
+    ar_send(6)
+
+    cp_gb = to_sib(s.gm, s.GB.at[myrows])
+
+    @pl.when(c == 0)
+    def _():
+        cp_gb.start()
+
+    both_waits(cp_gb, 0)
+
+    @pl.when(c == 1)
+    def _():
+        piece(s.J2X, 2, s.GB, s.st2)
+        plane_send(1, s.st2, 2, s.pr2)
+
+    res = ar_recv(6)
+    back_params(res, 1536, s.bnr, 512)
+
+    def grad_right(i, _):
+        val = grad_of(s.dr[rows16(i), :], s.yr[rows16(i), :], s.bnr, valid_at(i)).astype(BF)
+        s.gr[rows16(i), :] = val
+
+        return 0
+
+    tiles(16, grad_right)
+
+    def back_one(h, _):
+        cols = pl.ds(al(h * 256, 256), 256)
+        acc = mm_nt(s.glb[...], s.wl[cols, :]) + mm_nt(s.gr[...], s.wr[cols, :])
+        gz = s.d1[:, cols] * acc
+        s.d1[:, cols] = gz
+        xh = s.y1[:, cols] * s.bn0[2:3, cols] + s.bn0[3:4, cols]
+        st[7][0:1, cols] = jnp.sum(gz, axis=0, keepdims=True)
+        st[7][1:2, cols] = jnp.sum(gz * xh, axis=0, keepdims=True)
+        return 0
+
+    lax.fori_loop(0, 4, back_one, 0)
+    ar_send(7)
+
+    @pl.when(c == 1)
+    def _():
+        s.GA[myrows, :] = s.gr[...]
+
+    cp_gr = to_sib(s.gr, s.GA.at[myrows])
+
+    @pl.when(c == 0)
+    def _():
+        cp_gr.start()
+
+    both_waits(cp_gr, 0)
+
+    @pl.when(c == 1)
+    def _():
+        for k in (0, 1):
+            piece(s.J2X, k, s.GA, s.st2)
+            plane_send(1, s.st2, k, s.pr2)
+
+    res = ar_recv(7)
+    back_params(res, 0, s.bn0, 1024)
+
+    def grad_one(i, _):
+        val = grad_of(s.d1[rows16(i), :], s.y1[rows16(i), :], s.bn0, valid_at(i))
+        low = val.astype(BF)
+        s.G0[rows16(i), :] = low
+        s.Gall[pl.ds(al(own8 * 256 + i * 16, 16), 16), :] = low
+        return 0
+
+    tiles(16, grad_one)
+
+    halo_up(7, s.G0.at[pl.ds(0, 128)], s.G0.at[pl.ds(256, 128)])
+
+    def g_block(core, batch, q):
+        return s.Gall.at[pl.ds(al((core * 4 + batch) * 256, 256), 256), pl.ds(q * 256, 256)]
+
+    def g_direct(q, j):
+        return remote(
+            g_block(c, b, q), g_block(c, b, q), s.gs.at[q, j - 1], s.grs.at[q, j - 1], (r, (b + j) % 4)
+        )
+
+    def g_forward(q, j):
+        blk = g_block(c, (b - j + 4) % 4, q)
+        return remote(blk, blk, s.gfs.at[q, j], s.gfr.at[q, j], sib)
+
+    for q in range(4):
+        for j in (1, 2, 3):
+            g_direct(q, j).start()
+    for q in range(4):
+        g_forward(q, 0).start()
+
+    for dc in range(2):
+        for db in range(4):
+            if dc or db:
+                idx = dc * 4 + db
+                src8 = ((c + dc) % 2) * 4 + (b - db + 4) % 4
+                for k in range(3):
+                    dst = s.XG.at[k, :, pl.ds(al(src8 * 256, 256), 256)]
+                    if k < 2:
+                        recv_wait(dst, s.xr.at[k, idx])
+                    else:
+
+                        @pl.when(jnp.logical_and(c == 0, y == 0))
+                        def _():
+                            recv_wait(dst, s.xr.at[k, idx])
+
+    def chain(zp, q, own, down_job):
+        up_to = (r + 2, b)
+        down_to = (r - 2, b)
+        own()
+
+        if zp > 0:
+
+            @pl.when(jnp.logical_and(z > 0, z <= zp))
+            def _():
+                slot = s.zb.at[zp - 1, q]
+                recv_wait(slot, s.zur.at[zp, q])
+                s.tile[...] = s.tile[...] + slot[...].astype(F32)
+
+        if zp < 3:
+
+            @pl.when(jnp.logical_and(z < 3, z >= zp))
+            def _():
+                slot = s.za.at[zp, q]
+                recv_wait(slot, s.zdr.at[zp, q])
+                s.tile[...] = s.tile[...] + slot[...].astype(F32)
+
+        if zp > 0:
+
+            @pl.when(z < zp)
+            def _():
+                s.zs[zp, q] = s.tile[...].astype(BF)
+                remote(s.zs.at[zp, q], s.zb.at[zp - 1, q], s.zus.at[zp, q], s.zur.at[zp, q], up_to).start()
+
+        if zp < 3:
+
+            @pl.when(z > zp)
+            def _():
+                s.zs[zp, q] = s.tile[...].astype(BF)
+                remote(s.zs.at[zp, q], s.za.at[zp, q], s.zds.at[zp, q], s.zdr.at[zp, q], down_to).start()
+
+        def final_down():
+            for h in range(2):
+                s.wgo[pl.ds(2 * q + h, 256, stride=8), :] = s.tile[:, h * 128 : h * 128 + 128]
+
+        def final_tile():
+            mi, ni = q // 2, q % 2
+            for h in range(2):
+                s.wgo[pl.ds(mi * 1024 + ni * 2 + h, 256, stride=4), :] = s.tile[:, h * 128 : h * 128 + 128]
+
+        @pl.when(z == zp)
+        def _():
+            if down_job is True:
+                final_down()
+            elif down_job is False:
+                final_tile()
+            else:
+                pl.when(down_job)(final_down)
+                pl.when(jnp.logical_not(down_job))(final_tile)
+
+    def chain_drain(zp, q):
+        if zp > 0:
+
+            @pl.when(z < zp)
+            def _():
+                pltpu.make_async_copy(s.zs.at[zp, q], s.zs.at[zp, q], s.zus.at[zp, q]).wait()
+
+        if zp < 3:
+
+            @pl.when(z > zp)
+            def _():
+                pltpu.make_async_copy(s.zs.at[zp, q], s.zs.at[zp, q], s.zds.at[zp, q]).wait()
+
+    def own_plane(stage, slots, q):
+        rows = pl.ds((q // 2) * 256, 256)
+        cols = pl.ds((q % 2) * 256, 256)
+
+        def go():
+            v = stage[b, rows, cols].astype(F32)
+            for j in range(3):
+                v = v + slots[j, rows, cols].astype(F32)
+            s.tile[...] = v
+
+        return go
+
+    def own_down(k, q):
+        def go():
+            s.tile[...] = mm(s.XG[k], s.Gall[:, pl.ds(q * 256, 256)])
+
+        return go
+
+    for j in range(3):
+        recv_wait(s.pr3.at[j], s.pr.at[0, j])
+    for q in range(4):
+        chain(3, q, own_plane(st3, s.pr3, q), False)
+
+    is_tap8 = jnp.logical_and(c == 0, y == 0)
+    has_plane2 = jnp.logical_not(is_tap8)
+
+    @pl.when(has_plane2)
+    def _():
+        for j in range(3):
+            recv_wait(s.pr2.at[j], s.pr.at[1, j])
+
+    for q in range(4):
+        for j in (1, 2, 3):
+            recv_wait(g_block(c, (b - j + 4) % 4, q), s.grs.at[q, j - 1])
+            g_forward(q, j).start()
+        for j in range(4):
+            recv_wait(g_block(1 - c, (b - j + 4) % 4, q), s.gfr.at[q, j])
+        chain(0, q, own_down(0, q), True)
+        chain(1, q, own_down(1, q), True)
+
+        def own_two():
+            pl.when(is_tap8)(own_down(2, q))
+            pl.when(has_plane2)(own_plane(s.st2, s.pr2, q))
+
+        chain(2, q, own_two, is_tap8)
+
+    store(s.wgo, wg_ref)
+
+    halo_up_wait(7, s.G0.at[pl.ds(256, 128)])
+
+    def shift_one(i, _):
+        n = i % 8
+        for h in range(2):
+            cols = pl.ds(h * 512, 512)
+            s.pad[n, 8:24, :] = s.G0[rows16(i), cols].astype(F32)
+            s.Gp[rows16(i), cols] = s.pad[n, 9:25, :].astype(BF)
+        return 0
+
+    lax.fori_loop(0, 24, shift_one, 0)
+
+    def back_conv(h, _):
+        ch = pl.ds(al(h * 256, 256), 256)
+
+        def part(src, row, tap):
+            return mm_nt(src[pl.ds(row * 128, 256), :], s.wd[tap, ch, :])
+
+        for par in range(2):
+            if par == 0:
+                even = part(s.G0, 0, 4)
+                odd = part(s.G0, 0, 5) + part(s.Gp, 0, 3)
+            else:
+                even = part(s.G0, 0, 7) + part(s.G0, 1, 1)
+                odd = (part(s.G0, 0, 8) + part(s.Gp, 0, 6)) + (part(s.G0, 1, 2) + part(s.Gp, 1, 0))
+            for q in range(2):
+                s.igf[q, pl.ds(0, 256, stride=2), :] = even[:, q * 128 : q * 128 + 128]
+                s.igf[q, pl.ds(1, 256, stride=2), :] = odd[:, q * 128 : q * 128 + 128]
+            for rr in range(2):
+                for q in range(2):
+                    s.inraw[2 * rr + par, :, :, pl.ds(al(h * 256 + q * 128, 128), 128)] = (
+                        s.igf[q, rr * 256 : rr * 256 + 256, :].astype(BF).reshape(8, 32, 128)
+                    )
+        return 0
+
+    lax.fori_loop(0, 2, back_conv, 0)
+    for i in range(4):
+        store(s.inraw.at[i], ig_ref.at[:, i])
+
+    for q in range(4):
+        for zp in range(4):
+            chain_drain(zp, q)
+        for j in (1, 2, 3):
+            g_direct(q, j).wait_send()
+        for j in range(4):
+            g_forward(q, j).wait_send()
+    for k in range(4):
+
+        @pl.when(k != b)
+        def _():
+            pltpu.make_async_copy(st3.at[k], st3.at[k], s.ps.at[0, k]).wait()
+
+            @pl.when(jnp.logical_or(c == 1, k >= 2))
+            def _():
+                pltpu.make_async_copy(s.st2.at[k], s.st2.at[k], s.ps.at[1, k]).wait()
+
+    for cp in outs:
+        cp.wait()
+
+
+def fused_step(
+    inputs, counts, down_weight, left_weight, right_weight, reduce_weight, spread_weight,
+    norm_gains, norm_biases, running_mean, running_var, section_cotangent, block_cotangent,
+):
+    table = scratch_table()
+    names = tuple(table)
+    sds = jax.ShapeDtypeStruct
+    row = (1, 3072)
+    vmem = pl.BlockSpec(memory_space=pltpu.VMEM)
+    smem = pl.BlockSpec(memory_space=pltpu.SMEM)
+    hbm = pl.BlockSpec(memory_space=pl.ANY)
+    outs = pl.pallas_call(
+        functools.partial(fused_kernel, names, 13, 8),
+        out_shape=(
+            sds((8, 2, 16, 1024), BF),
+            sds((8, 2, 16, 512), BF),
+            sds((8, 4, 32, 512), BF),
+            sds((2048, 128), F32),
+            sds(row, F32),
+            sds(row, F32),
+            sds(row, F32),
+            sds(row, F32),
+        ),
+        in_specs=[hbm, smem, hbm, hbm, hbm, hbm, hbm, vmem, vmem, vmem, vmem, hbm, hbm],
+        out_specs=(hbm, hbm, hbm, hbm, vmem, vmem, vmem, vmem),
+        scratch_shapes=list(table.values()),
+        compiler_params=pltpu.CompilerParams(
+            collective_id=0, has_side_effects=True, vmem_limit_bytes=64 * 2**20 - 2**16
+        ),
+        cost_estimate=pl.CostEstimate(flops=13 * 10**9, bytes_accessed=21 * 10**6, transcendentals=10**6),
+    )(
+        inputs, counts, down_weight.reshape((9,) + down_weight.shape[2:]), left_weight, right_weight,
+        reduce_weight, spread_weight.reshape((9,) + spread_weight.shape[2:]),
+        norm_gains.reshape(row), norm_biases.reshape(row), running_mean.reshape(row), running_var.reshape(row),
+        section_cotangent, block_cotangent,
+    )
+    so, bo, ig, wg, gg, bg, nm, nv = outs
+    return (so, bo, ig, wg.reshape(-1), gg.reshape(-1), bg.reshape(-1), nm.reshape(-1), nv.reshape(-1))
+
+
+def fits_fused(mesh):
+    return dict(mesh.shape) == {"rows": 8, "batch": 4}
+
+
 def solution(mesh):
     placed = (
         P("batch", "rows", None, None),
@@ -280,7 +1356,7 @@
         P("batch", "rows", None, None),
     )
     return jax.shard_map(
-        on_device,
+        fused_step if fits_fused(mesh) else on_device,
         mesh=mesh,
         in_specs=placed,
         out_specs=(

time: 945 us -> 280 us (0.30); the launches traced: 933 us -> 279 us
  blocking collectives: 328 us -> 0 us
  waiting for transfers between devices: 328 us -> 0 us
  Pallas kernels: 0 us -> 265 us
  other arithmetic: 77.6 us -> 0 us
  matrix products: 74.2 us -> 0 us
  local copies, waits for them, and re-layouts: 86.9 us -> 13.3 us
  starting transfers between devices: 18.8 us -> 0 us
  between operations: 20.1 us -> 1.3 us
    psum x8 -> x0, blocking collectives: 328 us -> none  [the longest x5 198 us: norm_forward(): lax.psum((sum_first, sum_second, local_pixels), ('rows', 'batch'))]
    unnamed x4 -> x0, waiting for transfers between devices: 328 us -> none
    pallas_call x0 -> x1, Pallas kernels: none -> 265 us  [fused_step(): pl.pallas_call(functools.partial(fused_kernel, names, 13, 8), out_shape=(...]
    dot_general x63 -> x0, matrix products: 74.2 us -> none  [the longest x21 27.3 us: back_dot(): jnp.einsum('nhwd,cd->nhwc', left_op, right_op, preferred_element_type=jnp...]
    scatter-add x10 -> x0, other arithmetic: 43.9 us -> none  [the longest x9 42.8 us: on_device(): spread_back = spread_back.at[:, row_tap:row_tap + 2 * row_out:2, col_tap:...]
    slice x17 -> x0, local copies, waits for them, and re-layouts: 40.2 us -> none  [the longest x9 33 us: on_device(): padded[:, row_tap:row_tap + 2 * row_out:2, col_tap:col_tap + 2 * col_out:...]
    unnamed x218 -> x8, local copies, waits for them, and re-layouts: 36.3 us -> 13.3 us
    ppermute x6 -> x0, starting transfers between devices: 18.5 us -> none  [the longest x2 7.09 us: passed_along(): return lax.ppermute(block, axis, route)]
  transfers between devices with their start and end apart: 8 -> 0, of which waited for: 2 -> 0; matrix products, arithmetic and copies ran while one was open for 10% -> 0% of each run, Pallas kernels for 0% -> 0%
where the time goes in v1:
time: 280 us; the launch traced here: 279 us
  Pallas kernels  265 us (95%)
  local copies, waits for them, and re-layouts  13.3 us (5%)
    pallas_call x1, Pallas kernels, fused_step(): pl.pallas_call(functools.partial(fused_kernel, names, 13, 8), out_shape=(...  265 us
    unnamed x8, local copies, waits for them, and re-layouts  13.3 us

profile of v1, /device:TPU:17, one launch (start us, length us, event | category | flops | bytes accessed | tf_op | source)
XLA Modules:
  0.0 279.3 jit_solution(4009039546189752384)
XLA Ops:
  1.3 264.7 %shard_map.188 = (bf16[8,2,16,1024]{3,2,1,0:T(8,128)(2,1)}, bf16[8,2,16,512]{3,2,1,0:T(8,128)(2,1)}, bf16[8,4,32,512]{3,2,1,0:T(8,128)(2,1)}, f32[2048,128]{1,0:...) custom-call(bf16[8,4,32,512]{3,2,1,0:T(8,128)(2,1)} %refs_0_.1, ...), custom_call_target="tpu_custom_call" | custom-call | flops 12999999488 | bytes 21000000 | tf_op jit(solution)/shard_map/pallas_call | solution.py:1309
  266.0 1.9 copy.30
  267.9 1.7 copy.31
  269.5 2.3 copy.32
  271.8 2.3 copy.33
  274.1 1.3 copy.34
  275.4 1.3 copy.35
  276.7 1.3 copy.36
  278.0 1.3 copy.37

commit v2 on v1

--- a/solution.py
+++ b/solution.py
@@ -372,8 +372,8 @@
         xr=dma((3, 8)),
         bs=dma((12,)),
         br=dma((12,)),
-        ps=dma((2, 4)),
-        pr=dma((2, 3)),
+        ps=dma((2, 3, 2)),
+        pr=dma((2, 3, 2)),
         gs=dma((4, 3)),
         grs=dma((4, 3)),
         gfs=dma((4, 4)),
@@ -414,6 +414,7 @@
     own8 = c * 4 + b
     first = r == 0
     last = r == 7
+    plane = [b, b + 1 - 2 * x, b + 2 - 4 * y, 3 - b]
 
     def remote(src, dst, ss, rs, dev):
         return pltpu.make_async_remote_copy(
@@ -605,34 +606,35 @@
 
     lax.fori_loop(0, 9, xpose, 0)
 
-    def x_send(dc, db, do):
+    def x_copy(dc, j, k):
         cc = (c + dc) % 2
-        bb = (b + db) % 4
+        bb = plane[j]
         yy = bb // 2
         xx = bb % 2
-        idx = dc * 4 + db
         half = pl.ds(al(xx * 256, 256), 256)
         mine = pl.ds(al(own8 * 256, 256), 256)
-        for k in range(3):
-            tap = 2 * cc + yy + 4 * k if k < 2 else 8
-
-            def go():
-                src = s.xst.at[tap // 2, half, pl.ds(al((tap % 2) * 256, 256), 256)]
-                dst = s.XG.at[k, :, mine]
-                if dc == 0 and db == 0:
-                    cp = pltpu.make_async_copy(src, dst, s.xs.at[k, idx])
-                else:
-                    cp = remote(src, dst, s.xs.at[k, idx], s.xr.at[k, idx], ((z * 2 + cc), bb))
-                do(cp)
-
-            if k == 2:
-                pl.when(jnp.logical_and(cc == 0, yy == 0))(go)
-            else:
-                go()
-
-    for dc in range(2):
-        for db in range(4):
-            x_send(dc, db, lambda cp: cp.start())
+        tap = 2 * cc + yy + 4 * k if k < 2 else 8
+        src = s.xst.at[tap // 2, half, pl.ds(al((tap % 2) * 256, 256), 256)]
+        dst = s.XG.at[k, :, mine]
+        idx = dc * 4 + j
+        if dc == 0 and j == 0:
+            return pltpu.make_async_copy(src, dst, s.xs.at[k, idx])
+        return remote(src, dst, s.xs.at[k, idx], s.xr.at[k, idx], (z * 2 + cc, bb))
+
+    def x_when(dc, j, k, do):
+        if k < 2:
+            do()
+        else:
+            pl.when(jnp.logical_and((c + dc) % 2 == 0, plane[j] // 2 == 0))(do)
+
+    def x_start(js, ks):
+        for k in ks:
+            for dc in range(2):
+                for j in js:
+                    x_when(dc, j, k, lambda: x_copy(dc, j, k).start())
+
+    x_start((1, 2), (0,))
+    x_start((0,), (0, 1, 2))
 
     def norm_params(k, res, lo, bn, width):
         g = gain_ref[0:1, pl.ds(lo, width)]
@@ -700,6 +702,7 @@
 
     cp_act = to_sib(s.J2X.at[pl.ds(2 - 2 * c, 2), :, mycols], s.J2X.at[pl.ds(2 * c, 2), :, mycols])
     cp_act.start()
+    x_start((1, 2), (1,))
 
     res = ar_recv(1)
     norm_params(1, res[:, 0:512], 1024, s.bnl, 512)
@@ -724,6 +727,7 @@
     ar_send(2)
     halo_down(3, s.ym.at[pl.ds(256, 128)], s.ym.at[pl.ds(0, 128)])
     halo_up(4, s.ym.at[pl.ds(128, 128)], s.ym.at[pl.ds(384, 128)])
+    x_start((3,), (0,))
 
     loads["sc0"].wait()
     loads["sc1"].wait()
@@ -806,6 +810,7 @@
     ar_send(3)
     halo_down(5, s.y4.at[pl.ds(256, 128)], s.y4.at[pl.ds(0, 128)])
     halo_up(6, s.y4.at[pl.ds(128, 128)], s.y4.at[pl.ds(384, 128)])
+    x_start((3,), (1,))
 
     def slope_mid(i, _):
         zv = s.ym[pl.ds(al(128 + i * 16, 16), 16), :] * s.bnm[0:1, :] + s.bnm[1:2, :]
@@ -859,6 +864,7 @@
     st[4][0:1, 0:512] = jnp.sum(t1, axis=0, keepdims=True)
     st[4][1:2, 0:512] = jnp.sum(t2, axis=0, keepdims=True)
     ar_send(4)
+    x_start((1, 2, 3), (2,))
     for i in range(2):
         store(s.bo.at[i], bo_ref.at[:, i])
 
@@ -942,14 +948,15 @@
     both_waits(cp_m0, 0)
     cp_g4.wait()
 
-    def plane_send(job, stage, k, slots):
-        rel = (k - b + 4) % 4
-
-        @pl.when(rel > 0)
-        def _():
-            remote(
-                stage.at[k], slots.at[rel - 1], s.ps.at[job, k], s.pr.at[job, rel - 1], (r, k)
-            ).start()
+    def half_of(ref, k, hf):
+        return ref.at[k, pl.ds(hf * 256, 256)]
+
+    def plane_copy(job, j, hf):
+        stage, slots = ((st3, s.pr3), (s.st2, s.pr2))[job]
+        return remote(
+            half_of(stage, plane[j], hf), half_of(slots, j - 1, hf),
+            s.ps.at[job, j - 1, hf], s.pr.at[job, j - 1, hf], (r, plane[j]),
+        )
 
     def piece(lhs, k, rhs, stage):
         def body(i, _):
@@ -960,27 +967,22 @@
 
         lax.fori_loop(0, 4, body, 0)
 
-    for dc in range(2):
-        for db in range(4):
-            x_wait = lambda cp, me=(dc == 0 and db == 0): cp.wait() if me else cp.wait_send()
-            x_send(dc, db, x_wait)
+    for k in range(3):
+        for dc in range(2):
+            for j in range(4):
+                cp = x_copy(dc, j, k)
+                x_when(dc, j, k, cp.wait if dc == 0 and j == 0 else cp.wait_send)
     st3 = s.xst
-    for k in range(4):
-        piece(s.MT, k, s.G4, st3)
-        plane_send(0, st3, k, s.pr3)
-
-    both_waits(cp_ga, 1)
-
-    @pl.when(c == 0)
-    def _():
-        for k in (2, 3):
-            piece(s.J2X, k, s.GA, s.st2)
-            plane_send(1, s.st2, k, s.pr2)
-
-    @pl.when(c == 1)
-    def _():
-        piece(s.J2X, 3, s.G4, s.st2)
-        plane_send(1, s.st2, 3, s.pr2)
+
+    def piece3(j):
+        piece(s.MT, plane[j], s.G4, st3)
+
+    piece3(1)
+    piece3(2)
+    for j in (1, 2):
+        plane_copy(0, j, 0).start()
+    piece3(3)
+    piece3(0)
 
     res = ar_recv(5)
     back_params(res, 2048, s.bnm, 512)
@@ -1024,12 +1026,20 @@
     def _():
         cp_gb.start()
 
+    for j in (1, 2):
+        plane_copy(0, j, 1).start()
+    both_waits(cp_ga, 1)
     both_waits(cp_gb, 0)
+
+    @pl.when(c == 0)
+    def _():
+        for k in (2, 3):
+            piece(s.J2X, k, s.GA, s.st2)
 
     @pl.when(c == 1)
     def _():
+        piece(s.J2X, 3, s.G4, s.st2)
         piece(s.J2X, 2, s.GB, s.st2)
-        plane_send(1, s.st2, 2, s.pr2)
 
     res = ar_recv(6)
     back_params(res, 1536, s.bnr, 512)
@@ -1065,13 +1075,14 @@
     def _():
         cp_gr.start()
 
+    for hf in range(2):
+        plane_copy(0, 3, hf).start()
     both_waits(cp_gr, 0)
 
     @pl.when(c == 1)
     def _():
         for k in (0, 1):
             piece(s.J2X, k, s.GA, s.st2)
-            plane_send(1, s.st2, k, s.pr2)
 
     res = ar_recv(7)
     back_params(res, 0, s.bn0, 1024)
@@ -1088,91 +1099,107 @@
     halo_up(7, s.G0.at[pl.ds(0, 128)], s.G0.at[pl.ds(256, 128)])
 
     def g_block(core, batch, q):
-        return s.Gall.at[pl.ds(al((core * 4 + batch) * 256, 256), 256), pl.ds(q * 256, 256)]
+        return s.Gall.at[pl.ds(al((core * 4 + batch) * 256, 256), 256), pl.ds(al(q * 256, 256), 256)]
 
     def g_direct(q, j):
-        return remote(
-            g_block(c, b, q), g_block(c, b, q), s.gs.at[q, j - 1], s.grs.at[q, j - 1], (r, (b + j) % 4)
-        )
+        blk = g_block(c, b, q)
+        return remote(blk, blk, s.gs.at[q, j - 1], s.grs.at[q, j - 1], (r, plane[j]))
 
     def g_forward(q, j):
-        blk = g_block(c, (b - j + 4) % 4, q)
+        blk = g_block(c, plane[j], q)
         return remote(blk, blk, s.gfs.at[q, j], s.gfr.at[q, j], sib)
+
+    is_tap8 = jnp.logical_and(c == 0, y == 0)
+    has_plane2 = jnp.logical_not(is_tap8)
+
+    def to_piece_owner(j):
+        return jnp.logical_or(c == 1, plane[j] // 2 == 1)
 
     for q in range(4):
         for j in (1, 2, 3):
             g_direct(q, j).start()
-    for q in range(4):
         g_forward(q, 0).start()
+    for j in (1, 2, 3):
+
+        @pl.when(to_piece_owner(j))
+        def _():
+            for hf in range(2):
+                plane_copy(1, j, hf).start()
 
     for dc in range(2):
-        for db in range(4):
-            if dc or db:
-                idx = dc * 4 + db
-                src8 = ((c + dc) % 2) * 4 + (b - db + 4) % 4
+        for j in range(4):
+            if dc or j:
+                idx = dc * 4 + j
+                src8 = ((c + dc) % 2) * 4 + plane[j]
                 for k in range(3):
                     dst = s.XG.at[k, :, pl.ds(al(src8 * 256, 256), 256)]
+                    x_got = lambda: recv_wait(dst, s.xr.at[k, idx])
                     if k < 2:
-                        recv_wait(dst, s.xr.at[k, idx])
+                        x_got()
                     else:
-
-                        @pl.when(jnp.logical_and(c == 0, y == 0))
-                        def _():
-                            recv_wait(dst, s.xr.at[k, idx])
-
-    def chain(zp, q, own, down_job):
-        up_to = (r + 2, b)
-        down_to = (r - 2, b)
-        own()
-
-        if zp > 0:
-
-            @pl.when(jnp.logical_and(z > 0, z <= zp))
+                        pl.when(is_tap8)(x_got)
+
+    def chain(zp, slot, own, down_job):
+        far = max(zp, 3 - zp)
+        lag = jnp.where(z < zp, z, jnp.where(z > zp, 3 - z, far))
+        q = slot - lag
+
+        @pl.when(jnp.logical_and(q >= 0, q < 4))
+        def _():
+            own(q)
+            if zp > 0:
+
+                @pl.when(jnp.logical_and(z > 0, z <= zp))
+                def _():
+                    got = s.zb.at[zp - 1, q]
+                    recv_wait(got, s.zur.at[zp, q])
+                    s.tile[...] = s.tile[...] + got[...].astype(F32)
+
+            if zp < 3:
+
+                @pl.when(jnp.logical_and(z < 3, z >= zp))
+                def _():
+                    got = s.za.at[zp, q]
+                    recv_wait(got, s.zdr.at[zp, q])
+                    s.tile[...] = s.tile[...] + got[...].astype(F32)
+
+            if zp > 0:
+
+                @pl.when(z < zp)
+                def _():
+                    s.zs[zp, q] = s.tile[...].astype(BF)
+                    remote(
+                        s.zs.at[zp, q], s.zb.at[zp - 1, q], s.zus.at[zp, q], s.zur.at[zp, q], (r + 2, b)
+                    ).start()
+
+            if zp < 3:
+
+                @pl.when(z > zp)
+                def _():
+                    s.zs[zp, q] = s.tile[...].astype(BF)
+                    remote(
+                        s.zs.at[zp, q], s.za.at[zp, q], s.zds.at[zp, q], s.zdr.at[zp, q], (r - 2, b)
+                    ).start()
+
+            def final_down():
+                for h in range(2):
+                    s.wgo[pl.ds(2 * q + h, 256, stride=8), :] = s.tile[:, h * 128 : h * 128 + 128]
+
+            def final_tile():
+                for h in range(2):
+                    s.wgo[pl.ds((q // 2) * 1024 + (q % 2) * 2 + h, 256, stride=4), :] = s.tile[
+                        :, h * 128 : h * 128 + 128
+                    ]
+
+            @pl.when(z == zp)
             def _():
-                slot = s.zb.at[zp - 1, q]
-                recv_wait(slot, s.zur.at[zp, q])
-                s.tile[...] = s.tile[...] + slot[...].astype(F32)
-
-        if zp < 3:
-
-            @pl.when(jnp.logical_and(z < 3, z >= zp))
-            def _():
-                slot = s.za.at[zp, q]
-                recv_wait(slot, s.zdr.at[zp, q])
-                s.tile[...] = s.tile[...] + slot[...].astype(F32)
-
-        if zp > 0:
-
-            @pl.when(z < zp)
-            def _():
-                s.zs[zp, q] = s.tile[...].astype(BF)
-                remote(s.zs.at[zp, q], s.zb.at[zp - 1, q], s.zus.at[zp, q], s.zur.at[zp, q], up_to).start()
-
-        if zp < 3:
-
-            @pl.when(z > zp)
-            def _():
-                s.zs[zp, q] = s.tile[...].astype(BF)
-                remote(s.zs.at[zp, q], s.za.at[zp, q], s.zds.at[zp, q], s.zdr.at[zp, q], down_to).start()
-
-        def final_down():
-            for h in range(2):
-                s.wgo[pl.ds(2 * q + h, 256, stride=8), :] = s.tile[:, h * 128 : h * 128 + 128]
-
-        def final_tile():
-            mi, ni = q // 2, q % 2
-            for h in range(2):
-                s.wgo[pl.ds(mi * 1024 + ni * 2 + h, 256, stride=4), :] = s.tile[:, h * 128 : h * 128 + 128]
-
-        @pl.when(z == zp)
-        def _():
-            if down_job is True:
-                final_down()
-            elif down_job is False:
-                final_tile()
-            else:
-                pl.when(down_job)(final_down)
-                pl.when(jnp.logical_not(down_job))(final_tile)
+                if down_job is True:
+                    final_down()
+                elif down_job is False:
+                    final_tile()
+                else:
+                    pl.when(down_job)(final_down)
+                    pl.when(jnp.logical_not(down_job))(final_tile)
 
     def chain_drain(zp, q):
         if zp > 0:
@@ -1188,54 +1215,19 @@
                 pltpu.make_async_copy(s.zs.at[zp, q], s.zs.at[zp, q], s.zds.at[zp, q]).wait()
 
     def own_plane(stage, slots, q):
-        rows = pl.ds((q // 2) * 256, 256)
-        cols = pl.ds((q % 2) * 256, 256)
-
-        def go():
-            v = stage[b, rows, cols].astype(F32)
-            for j in range(3):
-                v = v + slots[j, rows, cols].astype(F32)
-            s.tile[...] = v
-
-        return go
+        rows = pl.ds(al((q // 2) * 256, 256), 256)
+        cols = pl.ds(al((q % 2) * 256, 256), 256)
+        v = stage[b, rows, cols].astype(F32)
+        for j in range(3):
+            v = v + slots[j, rows, cols].astype(F32)
+        s.tile[...] = v
 
     def own_down(k, q):
-        def go():
-            s.tile[...] = mm(s.XG[k], s.Gall[:, pl.ds(q * 256, 256)])
-
-        return go
-
-    for j in range(3):
-        recv_wait(s.pr3.at[j], s.pr.at[0, j])
-    for q in range(4):
-        chain(3, q, own_plane(st3, s.pr3, q), False)
-
-    is_tap8 = jnp.logical_and(c == 0, y == 0)
-    has_plane2 = jnp.logical_not(is_tap8)
-
-    @pl.when(has_plane2)
-    def _():
-        for j in range(3):
-            recv_wait(s.pr2.at[j], s.pr.at[1, j])
-
-    for q in range(4):
-        for j in (1, 2, 3):
-            recv_wait(g_block(c, (b - j + 4) % 4, q), s.grs.at[q, j - 1])
-            g_forward(q, j).start()
-        for j in range(4):
-            recv_wait(g_block(1 - c, (b - j + 4) % 4, q), s.gfr.at[q, j])
-        chain(0, q, own_down(0, q), True)
-        chain(1, q, own_down(1, q), True)
-
-        def own_two():
-            pl.when(is_tap8)(own_down(2, q))
-            pl.when(has_plane2)(own_plane(s.st2, s.pr2, q))
-
-        chain(2, q, own_two, is_tap8)
-
-    store(s.wgo, wg_ref)
-
-    halo_up_wait(7, s.G0.at[pl.ds(256, 128)])
+        s.tile[...] = mm(s.XG[k], s.Gall[:, pl.ds(al(q * 256, 256), 256)])
+
+    def own_two(q):
+        pl.when(is_tap8)(lambda: own_down(2, q))
+        pl.when(has_plane2)(lambda: own_plane(s.st2, s.pr2, q))
 
     def shift_one(i, _):
         n = i % 8
@@ -1245,32 +1237,69 @@
             s.Gp[rows16(i), cols] = s.pad[n, 9:25, :].astype(BF)
         return 0
 
-    lax.fori_loop(0, 24, shift_one, 0)
-
-    def back_conv(h, _):
+    lax.fori_loop(0, 16, shift_one, 0)
+
+    def back_conv(h, par):
         ch = pl.ds(al(h * 256, 256), 256)
 
         def part(src, row, tap):
             return mm_nt(src[pl.ds(row * 128, 256), :], s.wd[tap, ch, :])
 
-        for par in range(2):
-            if par == 0:
-                even = part(s.G0, 0, 4)
-                odd = part(s.G0, 0, 5) + part(s.Gp, 0, 3)
-            else:
-                even = part(s.G0, 0, 7) + part(s.G0, 1, 1)
-                odd = (part(s.G0, 0, 8) + part(s.Gp, 0, 6)) + (part(s.G0, 1, 2) + part(s.Gp, 1, 0))
+        if par == 0:
+            even = part(s.G0, 0, 4)
+            odd = part(s.G0, 0, 5) + part(s.Gp, 0, 3)
+        else:
+            even = part(s.G0, 0, 7) + part(s.G0, 1, 1)
+            odd = (part(s.G0, 0, 8) + part(s.Gp, 0, 6)) + (part(s.G0, 1, 2) + part(s.Gp, 1, 0))
+        for q in range(2):
+            s.igf[q, pl.ds(0, 256, stride=2), :] = even[:, q * 128 : q * 128 + 128]
+            s.igf[q, pl.ds(1, 256, stride=2), :] = odd[:, q * 128 : q * 128 + 128]
+        for rr in range(2):
             for q in range(2):
-                s.igf[q, pl.ds(0, 256, stride=2), :] = even[:, q * 128 : q * 128 + 128]
-                s.igf[q, pl.ds(1, 256, stride=2), :] = odd[:, q * 128 : q * 128 + 128]
-            for rr in range(2):
-                for q in range(2):
-                    s.inraw[2 * rr + par, :, :, pl.ds(al(h * 256 + q * 128, 128), 128)] = (
-                        s.igf[q, rr * 256 : rr * 256 + 256, :].astype(BF).reshape(8, 32, 128)
-                    )
-        return 0
-
-    lax.fori_loop(0, 2, back_conv, 0)
+                s.inraw[2 * rr + par, :, :, pl.ds(al(h * 256 + q * 128, 128), 128)] = (
+                    s.igf[q, rr * 256 : rr * 256 + 256, :].astype(BF).reshape(8, 32, 128)
+                )
+
+    def step(slot, _):
+        pl.when(slot < 2)(lambda: back_conv(slot, 0))
+
+        @pl.when(slot == 2)
+        def _():
+            halo_up_wait(7, s.G0.at[pl.ds(256, 128)])
+            lax.fori_loop(16, 24, shift_one, 0)
+
+        pl.when(jnp.logical_and(slot >= 2, slot < 4))(lambda: back_conv(slot - 2, 1))
+
+        @pl.when(slot < 4)
+        def _():
+            for j in (1, 2, 3):
+                recv_wait(g_block(c, plane[j], slot), s.grs.at[slot, j - 1])
+                g_forward(slot, j).start()
+            for j in range(4):
+                recv_wait(g_block(1 - c, plane[j], slot), s.gfr.at[slot, j])
+
+        chain(0, slot, lambda q: own_down(0, q), True)
+        chain(1, slot, lambda q: own_down(1, q), True)
+
+        @pl.when(slot == LATE3)
+        def _():
+            for j in (1, 2, 3):
+                for hf in range(2):
+                    recv_wait(half_of(s.pr3, j - 1, hf), s.pr.at[0, j - 1, hf])
+
+        chain(3, slot - LATE3, lambda q: own_plane(st3, s.pr3, q), False)
+
+        @pl.when(jnp.logical_and(slot == LATE2, has_plane2))
+        def _():
+            for j in (1, 2, 3):
+                for hf in range(2):
+                    recv_wait(half_of(s.pr2, j - 1, hf), s.pr.at[1, j - 1, hf])
+
+        chain(2, slot - jnp.where(is_tap8, 0, LATE2), own_two, is_tap8)
+        return 0
+
+    lax.fori_loop(0, 7 + max(LATE2 - 1, LATE3), step, 0)
+    store(s.wgo, wg_ref)
     for i in range(4):
         store(s.inraw.at[i], ig_ref.at[:, i])
 
@@ -1281,17 +1310,29 @@
             g_direct(q, j).wait_send()
         for j in range(4):
             g_forward(q, j).wait_send()
-    for k in range(4):
-
-        @pl.when(k != b)
-        def _():
-            pltpu.make_async_copy(st3.at[k], st3.at[k], s.ps.at[0, k]).wait()
-
-            @pl.when(jnp.logical_or(c == 1, k >= 2))
-            def _():
-                pltpu.make_async_copy(s.st2.at[k], s.st2.at[k], s.ps.at[1, k]).wait()
-
+    for j in (1, 2, 3):
+        for hf in range(2):
+            plane_copy(0, j, hf).wait_send()
+            pl.when(to_piece_owner(j))(lambda: plane_copy(1, j, hf).wait_send())
     for cp in outs:
+        cp.wait()
+
+
+LATE3 = 1
+LATE2 = 4
+
+
+def hand_over(n, *refs):
+    ins, outs, held = refs[:n], refs[n : 2 * n], refs[2 * n : 3 * n]
+    sems = refs[3 * n]
+    got = [pltpu.make_async_copy(ins[i], held[i], sems.at[0, i]) for i in range(n)]
+    put = [pltpu.make_async_copy(held[i], outs[i], sems.at[1, i]) for i in range(n)]
+    for cp in got:
+        cp.start()
+    for i in range(n):
+        got[i].wait()
+        put[i].start()
+    for cp in put:
         cp.wait()
 
 
@@ -1331,7 +1372,15 @@
         norm_gains.reshape(row), norm_biases.reshape(row), running_mean.reshape(row), running_var.reshape(row),
         section_cotangent, block_cotangent,
     )
-    so, bo, ig, wg, gg, bg, nm, nv = outs
+    n = len(outs)
+    so, bo, ig, wg, gg, bg, nm, nv = pl.pallas_call(
+        functools.partial(hand_over, n),
+        out_shape=tuple(sds(o.shape, o.dtype) for o in outs),
+        in_specs=[hbm] * n,
+        out_specs=(hbm,) * n,
+        scratch_shapes=[pltpu.VMEM(o.shape, o.dtype) for o in outs] + [pltpu.SemaphoreType.DMA((2, n))],
+        cost_estimate=pl.CostEstimate(flops=0, bytes_accessed=6 * 10**6, transcendentals=0),
+    )(*outs)
     return (so, bo, ig, wg.reshape(-1), gg.reshape(-1), bg.reshape(-1), nm.reshape(-1), nv.reshape(-1))
 
 

time: 280 us -> 158 us (0.56)
  the two profiles are of different devices: /device:TPU:17 before, /device:TPU:20 now
where the time goes in v2:
time: 158 us; the launch traced here: 157 us
  Pallas kernels  156 us (99%)
    pallas_call x1, Pallas kernels, fused_step(): pl.pallas_call(functools.partial(fused_kernel, names, 13, 8), out_shape=(...  153 us

profile of v2, /device:TPU:20, one launch (start us, length us, event | category | flops | bytes accessed | tf_op | source)
XLA Modules:
  0.0 157.5 jit_solution(5334912691757889085)
XLA Ops:
  1.3 153.3 %shard_map.188 = (bf16[8,2,16,1024]{3,2,1,0:T(8,128)(2,1)}, bf16[8,2,16,512]{3,2,1,0:T(8,128)(2,1)}, bf16[8,4,32,512]{3,2,1,0:T(8,128)(2,1)}, f32[2048,128]{1,0:...) custom-call(bf16[8,4,32,512]{3,2,1,0:T(8,128)(2,1)} %refs_0_.1, ...), custom_call_target="tpu_custom_call" | custom-call | flops 12999999488 | bytes 21000000 | tf_op jit(solution)/shard_map/pallas_call | solution.py:1350
  154.5 2.9 %shard_map.189 = (bf16[8,2,16,1024]{3,2,1,0:T(8,128)(2,1)}, bf16[8,2,16,512]{3,2,1,0:T(8,128)(2,1)}, bf16[8,4,32,512]{3,2,1,0:T(8,128)(2,1)}, f32[2048,128]{1,0:...) custom-call(bf16[8,2,16,1024]{3,2,1,0:T(8,128)(2,1)} %get-tuple-element.24.refs_0_, ...), custom_call_target="tpu_custom_call" | custom-call | bytes 6000000 | tf_op jit(solution)/shard_map/pallas_call | solution.py:1376

commit v3 on v2

--- a/solution.py
+++ b/solution.py
@@ -352,7 +352,6 @@
         zb=v((3, 4, 256, 256), BF),
         za=v((3, 4, 256, 256), BF),
         zs=v((4, 4, 256, 256), BF),
-        tile=v((256, 256), F32),
         wgo=v((2048, 128), F32),
         bn0=v((8, 1024), F32),
         bnl=v((8, 512), F32),
@@ -372,16 +371,16 @@
         xr=dma((3, 8)),
         bs=dma((12,)),
         br=dma((12,)),
-        ps=dma((2, 3, 2)),
-        pr=dma((2, 3, 2)),
+        ps=dma((2, 2, 3)),
+        pr=dma((2, 2, 3)),
         gs=dma((4, 3)),
         grs=dma((4, 3)),
         gfs=dma((4, 4)),
         gfr=dma((4, 4)),
-        zus=dma((4, 4)),
-        zur=dma((4, 4)),
-        zds=dma((4, 4)),
-        zdr=dma((4, 4)),
+        zus=dma((4, 8)),
+        zur=dma((4, 8)),
+        zds=dma((4, 8)),
+        zdr=dma((4, 8)),
     )
     widths = AR_WIDTHS
     for k, w in enumerate(widths):
@@ -391,7 +390,7 @@
     return table
 
 
-AR_WIDTHS = (1152, 1024, 512, 512, 1024, 512, 512, 1024)
+AR_WIDTHS = (1152, 1024, 512, 1024, 512, 512, 512, 1024)
 
 
 def fused_kernel(names, n_in, n_out, *refs):
@@ -472,8 +471,6 @@
         s.y4[384:512, :] = jnp.zeros((128, 512), F32)
         s.G0[256:384, :] = jnp.zeros((128, 1024), BF)
 
-    pl.semaphore_wait(bar, 31)
-
     nxt = (r + 1, b)
     prv = (r - 1, b)
 
@@ -504,10 +501,6 @@
         @pl.when(r < 7)
         def _():
             recv_wait(dst, s.hr.at[k])
-
-    halo_down(0, in_ref.at[:, 3], s.inraw.at[0])
-    halo_down(1, bc_ref.at[:, 1], s.bc.at[0])
-    halo_up(2, bc_ref.at[:, 0], s.bc.at[3])
 
     count = cnt_ref[0]
     vs = [(jnp.int32(n) < count).astype(F32) for n in range(8)]
@@ -566,6 +559,10 @@
     for i in range(4):
         loads["in%d" % i].wait()
         deinterleave(1 + i)
+    pl.semaphore_wait(bar, 31)
+    halo_down(0, in_ref.at[:, 3], s.inraw.at[0])
+    halo_down(1, bc_ref.at[:, 1], s.bc.at[0])
+    halo_up(2, bc_ref.at[:, 0], s.bc.at[3])
     for t in (3, 4, 5, 6, 7, 8):
         loads["wd%d" % t].wait()
 
@@ -750,8 +747,8 @@
 
     zero16 = jnp.zeros((16, 512), F32)
     t1, t2 = tiles(16, left_branch, (zero16, zero16), unroll=1)
-    st[4][0:1, 512:1024] = jnp.sum(t1, axis=0, keepdims=True)
-    st[4][1:2, 512:1024] = jnp.sum(t2, axis=0, keepdims=True)
+    st[3][0:1, 512:1024] = jnp.sum(t1, axis=0, keepdims=True)
+    st[3][1:2, 512:1024] = jnp.sum(t2, axis=0, keepdims=True)
     outs = []
 
     def store(src, dst):
@@ -844,8 +841,20 @@
     halo_down_wait(1, s.bc.at[0])
     halo_up_wait(2, s.bc.at[3])
 
+    def back_params(res, lo, bn, width):
+        inv_t = s.tot[0:1, 0:width]
+        bg_ref[0:1, pl.ds(lo, width)] = res[0:1]
+        gg_ref[0:1, pl.ds(lo, width)] = res[1:2]
+        bn[4:5, :] = res[0:1] * inv_t
+        bn[5:6, :] = res[1:2] * inv_t
+
+    def grad_of(gz, yv, bn, v):
+        xh = yv * bn[2:3, :] + bn[3:4, :]
+        return bn[0:1, :] * (gz - v * (bn[4:5, :] + xh * bn[5:6, :]))
+
     res = ar_recv(3)
-    norm_params(4, res, 2560, s.bn4, 512)
+    norm_params(4, res[:, 0:512], 2560, s.bn4, 512)
+    back_params(res[:, 512:1024], 1024, s.bnl, 512)
 
     def norm_four(i, carry):
         t1, t2 = carry
@@ -861,10 +870,103 @@
         return t1 + gz, t2 + gx
 
     t1, t2 = tiles(16, norm_four, (zero16, zero16), unroll=1)
-    st[4][0:1, 0:512] = jnp.sum(t1, axis=0, keepdims=True)
-    st[4][1:2, 0:512] = jnp.sum(t2, axis=0, keepdims=True)
+    st[4][0:1, :] = jnp.sum(t1, axis=0, keepdims=True)
+    st[4][1:2, :] = jnp.sum(t2, axis=0, keepdims=True)
     ar_send(4)
     x_start((1, 2, 3), (2,))
+    myrows = pl.ds(al(c * 256, 256), 256)
+    st3 = s.xst
+
+    def grad_left(i, _):
+        val = grad_of(s.gl[rows16(i), :], s.yl[rows16(i), :], s.bnl, valid_at(i)).astype(BF)
+        s.glb[rows16(i), :] = val
+        s.GA[pl.ds(al(c * 256 + i * 16, 16), 16), :] = val
+        return 0
+
+    tiles(16, grad_left)
+    cp_ga = to_sib(s.glb, s.GA.at[myrows])
+
+    @pl.when(c == 1)
+    def _():
+        cp_ga.start()
+
+    def both_waits(cp, sender):
+        pl.when(c == sender)(cp.wait_send)
+        pl.when(c != sender)(cp.wait_recv)
+
+    def half_of(ref, k, hf):
+        return ref.at[k, pl.ds(hf * 256, 256)]
+
+    def owned(job, j):
+        return True if job == 0 else jnp.logical_or(c == 1, plane[j] // 2 == 1)
+
+    def when_owned(job, j, do):
+        if job == 0:
+            do()
+        else:
+            pl.when(owned(job, j))(do)
+
+    def plane_copy(job, hf, m):
+        stage, slots = ((st3, s.pr3), (s.st2, s.pr2))[job]
+        near, far = ((1, 2), (2, 1))[hf]
+        src = (near, 3, far)[m]
+        to = (near, near, far)[m]
+        cp = remote(
+            half_of(stage, plane[src], hf), half_of(slots, m, hf), s.ps.at[job, hf, m], s.pr.at[job, hf, m],
+            (r, plane[to]),
+        )
+        return cp, src, (0, far, 0)[m]
+
+    def plane_start(job, hf, m):
+        cp, src, _ = plane_copy(job, hf, m)
+        when_owned(job, src, cp.start)
+
+    def plane_got(job, hf, m):
+        cp, _, mine_at = plane_copy(job, hf, m)
+        when_owned(job, mine_at, cp.wait_recv)
+
+    def plane_sent(job, hf, m):
+        cp, src, _ = plane_copy(job, hf, m)
+        when_owned(job, src, cp.wait_send)
+
+    def plane_second(job, hf):
+        stage, slots = ((st3, s.pr3), (s.st2, s.pr2))[job]
+        far = (2, 1)[hf]
+        plane_got(job, hf, 1)
+
+        def add():
+            def body(i, _):
+                rows = pl.ds(al(hf * 256 + i * 16, 16), 16)
+                k = plane[far]
+                stage[k, rows, :] = (stage[k, rows, :].astype(F32) + slots[1, rows, :].astype(F32)).astype(BF)
+                return 0
+
+            lax.fori_loop(0, 16, body, 0)
+
+        when_owned(job, far, add)
+        plane_start(job, hf, 2)
+
+    def piece(lhs, k, rhs, stage):
+        def body(i, _):
+            rows = pl.ds(al((i // 2) * 256, 256), 256)
+            cols = pl.ds(al((i % 2) * 256, 256), 256)
+            stage[k, rows, cols] = mm(lhs[k, rows, :], rhs[:, cols]).astype(BF)
+            return 0
+
+        lax.fori_loop(0, 4, body, 0)
+
+    cp_act.wait()
+    cp_mt.wait()
+    both_waits(cp_ga, 1)
+
+    @pl.when(c == 0)
+    def _():
+        for k in (2, 3):
+            piece(s.J2X, k, s.GA, s.st2)
+        for m in (1, 0):
+            for hf in range(2):
+                plane_start(1, hf, m)
+
     for i in range(2):
         store(s.bo.at[i], bo_ref.at[:, i])
 
@@ -880,20 +982,8 @@
 
     tiles(16, halo_four)
 
-    def back_params(res, lo, bn, width):
-        inv_t = s.tot[0:1, 0:width]
-        bg_ref[0:1, pl.ds(lo, width)] = res[0:1]
-        gg_ref[0:1, pl.ds(lo, width)] = res[1:2]
-        bn[4:5, :] = res[0:1] * inv_t
-        bn[5:6, :] = res[1:2] * inv_t
-
-    def grad_of(gz, yv, bn, v):
-        xh = yv * bn[2:3, :] + bn[3:4, :]
-        return bn[0:1, :] * (gz - v * (bn[4:5, :] + xh * bn[5:6, :]))
-
     res = ar_recv(4)
-    back_params(res[:, 0:512], 2560, s.bn4, 512)
-    back_params(res[:, 512:1024], 1024, s.bnl, 512)
+    back_params(res, 2560, s.bn4, 512)
 
     def grad_four(i, _):
         v = valid_at(i) * edge_at(i)
@@ -921,68 +1011,33 @@
     lax.fori_loop(0, 2, back_four, 0)
     ar_send(5)
 
-    def grad_left(i, _):
-        val = grad_of(s.gl[rows16(i), :], s.yl[rows16(i), :], s.bnl, valid_at(i)).astype(BF)
-        s.glb[rows16(i), :] = val
-        s.GA[pl.ds(al(c * 256 + i * 16, 16), 16), :] = val
-        return 0
-
-    tiles(16, grad_left)
-    myrows = pl.ds(al(c * 256, 256), 256)
     s.G4[myrows, :] = s.X[640:896, :]
     cp_g4 = to_sib(s.G4.at[myrows], s.G4.at[myrows])
     cp_g4.start()
-    cp_ga = to_sib(s.glb, s.GA.at[myrows])
-
-    @pl.when(c == 1)
-    def _():
-        cp_ga.start()
-
-    def both_waits(cp, sender):
-        pl.when(c == sender)(cp.wait_send)
-        pl.when(c != sender)(cp.wait_recv)
-
-    cp_act.wait()
     both_waits(cp_low, 0)
-    cp_mt.wait()
     both_waits(cp_m0, 0)
     cp_g4.wait()
-
-    def half_of(ref, k, hf):
-        return ref.at[k, pl.ds(hf * 256, 256)]
-
-    def plane_copy(job, j, hf):
-        stage, slots = ((st3, s.pr3), (s.st2, s.pr2))[job]
-        return remote(
-            half_of(stage, plane[j], hf), half_of(slots, j - 1, hf),
-            s.ps.at[job, j - 1, hf], s.pr.at[job, j - 1, hf], (r, plane[j]),
-        )
-
-    def piece(lhs, k, rhs, stage):
-        def body(i, _):
-            rows = pl.ds(al((i // 2) * 256, 256), 256)
-            cols = pl.ds(al((i % 2) * 256, 256), 256)
-            stage[k, rows, cols] = mm(lhs[k, rows, :], rhs[:, cols]).astype(BF)
-            return 0
-
-        lax.fori_loop(0, 4, body, 0)
 
     for k in range(3):
         for dc in range(2):
             for j in range(4):
                 cp = x_copy(dc, j, k)
                 x_when(dc, j, k, cp.wait if dc == 0 and j == 0 else cp.wait_send)
-    st3 = s.xst
 
     def piece3(j):
         piece(s.MT, plane[j], s.G4, st3)
 
+    piece3(3)
+    for hf in range(2):
+        plane_start(0, hf, 1)
+
+    @pl.when(c == 0)
+    def _():
+        for hf in range(2):
+            plane_second(1, hf)
+
     piece3(1)
     piece3(2)
-    for j in (1, 2):
-        plane_copy(0, j, 0).start()
-    piece3(3)
-    piece3(0)
 
     res = ar_recv(5)
     back_params(res, 2048, s.bnm, 512)
@@ -1026,15 +1081,10 @@
     def _():
         cp_gb.start()
 
-    for j in (1, 2):
-        plane_copy(0, j, 1).start()
-    both_waits(cp_ga, 1)
+    for hf in range(2):
+        plane_start(0, hf, 0)
+    piece3(0)
     both_waits(cp_gb, 0)
-
-    @pl.when(c == 0)
-    def _():
-        for k in (2, 3):
-            piece(s.J2X, k, s.GA, s.st2)
 
     @pl.when(c == 1)
     def _():
@@ -1076,7 +1126,7 @@
         cp_gr.start()
 
     for hf in range(2):
-        plane_copy(0, 3, hf).start()
+        plane_second(0, hf)
     both_waits(cp_gr, 0)
 
     @pl.when(c == 1)
@@ -1112,19 +1162,18 @@
     is_tap8 = jnp.logical_and(c == 0, y == 0)
     has_plane2 = jnp.logical_not(is_tap8)
 
-    def to_piece_owner(j):
-        return jnp.logical_or(c == 1, plane[j] // 2 == 1)
-
     for q in range(4):
         for j in (1, 2, 3):
             g_direct(q, j).start()
         g_forward(q, 0).start()
-    for j in (1, 2, 3):
-
-        @pl.when(to_piece_owner(j))
-        def _():
-            for hf in range(2):
-                plane_copy(1, j, hf).start()
+        if q == 3:
+
+            @pl.when(c == 1)
+            def _():
+                for m in (1, 0):
+                    for hf in range(2):
+                        plane_start(1, hf, m)
+
 
     for dc in range(2):
         for j in range(4):
@@ -1139,95 +1188,99 @@
                     else:
                         pl.when(is_tap8)(x_got)
 
-    def chain(zp, slot, own, down_job):
-        far = max(zp, 3 - zp)
-        lag = jnp.where(z < zp, z, jnp.where(z > zp, 3 - z, far))
-        q = slot - lag
-
-        @pl.when(jnp.logical_and(q >= 0, q < 4))
+    def half_tile(ref, k, q, h):
+        return ref.at[k, q, pl.ds(h * 128, 128)]
+
+    def chain(zp, q, own, put, here):
+        @pl.when(jnp.logical_and(here, jnp.logical_and(q >= 0, q < 4)))
         def _():
-            own(q)
+            val = own(q)
+
+            def below(h):
+                got = half_tile(s.zb, zp - 1, q, h)
+                recv_wait(got, s.zur.at[zp, 2 * q + h])
+                return got[...].astype(F32)
+
+            def above(h):
+                got = half_tile(s.za, zp, q, h)
+                recv_wait(got, s.zdr.at[zp, 2 * q + h])
+                return got[...].astype(F32)
+
+            def mine(h):
+                return val[h * 128 : h * 128 + 128]
+
+            def up(h, v):
+                part = half_tile(s.zs, zp, q, h)
+                part[...] = v.astype(BF)
+                there = half_tile(s.zb, zp - 1, q, h)
+                remote(part, there, s.zus.at[zp, 2 * q + h], s.zur.at[zp, 2 * q + h], (r + 2, b)).start()
+
+            def down(h, v):
+                part = half_tile(s.zs, zp, q, h)
+                part[...] = v.astype(BF)
+                there = half_tile(s.za, zp, q, h)
+                remote(part, there, s.zds.at[zp, 2 * q + h], s.zdr.at[zp, 2 * q + h], (r - 2, b)).start()
+
+            def each(do):
+                def both():
+                    for h in range(2):
+                        do(h)
+
+                return both
+
             if zp > 0:
-
-                @pl.when(jnp.logical_and(z > 0, z <= zp))
-                def _():
-                    got = s.zb.at[zp - 1, q]
-                    recv_wait(got, s.zur.at[zp, q])
-                    s.tile[...] = s.tile[...] + got[...].astype(F32)
-
+                pl.when(z == 0)(each(lambda h: up(h, mine(h))))
+            if zp > 1:
+                pl.when(jnp.logical_and(z > 0, z < zp))(each(lambda h: up(h, mine(h) + below(h))))
             if zp < 3:
-
-                @pl.when(jnp.logical_and(z < 3, z >= zp))
-                def _():
-                    got = s.za.at[zp, q]
-                    recv_wait(got, s.zdr.at[zp, q])
-                    s.tile[...] = s.tile[...] + got[...].astype(F32)
-
+                pl.when(z == 3)(each(lambda h: down(h, mine(h))))
+            if zp < 2:
+                pl.when(jnp.logical_and(z > zp, z < 3))(each(lambda h: down(h, mine(h) + above(h))))
+
+            @pl.when(z == zp)
+            def _():
+                for h in range(2):
+                    v = mine(h)
+                    if zp > 0:
+                        v = v + below(h)
+                    if zp < 3:
+                        v = v + above(h)
+                    put(q, h, v)
+
+    def put_down(q, h, v):
+        for i in range(2):
+            s.wgo[pl.ds(h * 1024 + 2 * q + i, 128, stride=8), :] = v[:, i * 128 : i * 128 + 128]
+
+    def put_tile(q, h, v):
+        base = (q // 2) * 1024 + h * 512 + (q % 2) * 2
+        for i in range(2):
+            s.wgo[pl.ds(base + i, 128, stride=4), :] = v[:, i * 128 : i * 128 + 128]
+
+    def chain_drain(zp, q):
+        for h in range(2):
+            part = half_tile(s.zs, zp, q, h)
             if zp > 0:
 
                 @pl.when(z < zp)
                 def _():
-                    s.zs[zp, q] = s.tile[...].astype(BF)
-                    remote(
-                        s.zs.at[zp, q], s.zb.at[zp - 1, q], s.zus.at[zp, q], s.zur.at[zp, q], (r + 2, b)
-                    ).start()
+                    pltpu.make_async_copy(part, part, s.zus.at[zp, 2 * q + h]).wait()
 
             if zp < 3:
 
                 @pl.when(z > zp)
                 def _():
-                    s.zs[zp, q] = s.tile[...].astype(BF)
-                    remote(
-                        s.zs.at[zp, q], s.za.at[zp, q], s.zds.at[zp, q], s.zdr.at[zp, q], (r - 2, b)
-                    ).start()
-
-            def final_down():
-                for h in range(2):
-                    s.wgo[pl.ds(2 * q + h, 256, stride=8), :] = s.tile[:, h * 128 : h * 128 + 128]
-
-            def final_tile():
-                for h in range(2):
-                    s.wgo[pl.ds((q // 2) * 1024 + (q % 2) * 2 + h, 256, stride=4), :] = s.tile[
-                        :, h * 128 : h * 128 + 128
-                    ]
-
-            @pl.when(z == zp)
-            def _():
-                if down_job is True:
-                    final_down()
-                elif down_job is False:
-                    final_tile()
-                else:
-                    pl.when(down_job)(final_down)
-                    pl.when(jnp.logical_not(down_job))(final_tile)
-
-    def chain_drain(zp, q):
-        if zp > 0:
-
-            @pl.when(z < zp)
-            def _():
-                pltpu.make_async_copy(s.zs.at[zp, q], s.zs.at[zp, q], s.zus.at[zp, q]).wait()
-
-        if zp < 3:
-
-            @pl.when(z > zp)
-            def _():
-                pltpu.make_async_copy(s.zs.at[zp, q], s.zs.at[zp, q], s.zds.at[zp, q]).wait()
+                    pltpu.make_async_copy(part, part, s.zds.at[zp, 2 * q + h]).wait()
 
     def own_plane(stage, slots, q):
         rows = pl.ds(al((q // 2) * 256, 256), 256)
         cols = pl.ds(al((q % 2) * 256, 256), 256)
         v = stage[b, rows, cols].astype(F32)
-        for j in range(3):
-            v = v + slots[j, rows, cols].astype(F32)
-        s.tile[...] = v
+        for m in (0, 2):
+            v = v + slots[m, rows, cols].astype(F32)
+        return v
 
     def own_down(k, q):
-        s.tile[...] = mm(s.XG[k], s.Gall[:, pl.ds(al(q * 256, 256), 256)])
-
-    def own_two(q):
-        pl.when(is_tap8)(lambda: own_down(2, q))
-        pl.when(has_plane2)(lambda: own_plane(s.st2, s.pr2, q))
+        return mm(s.XG[k], s.Gall[:, pl.ds(al(q * 256, 256), 256)])
 
     def shift_one(i, _):
         n = i % 8
@@ -1260,15 +1313,25 @@
                     s.igf[q, rr * 256 : rr * 256 + 256, :].astype(BF).reshape(8, 32, 128)
                 )
 
+    left2 = jnp.logical_and(c == 0, y == 1)
+    late2 = c == 1
+
     def step(slot, _):
         pl.when(slot < 2)(lambda: back_conv(slot, 0))
 
-        @pl.when(slot == 2)
+        @pl.when(slot == 0)
         def _():
-            halo_up_wait(7, s.G0.at[pl.ds(256, 128)])
-            lax.fori_loop(16, 24, shift_one, 0)
-
-        pl.when(jnp.logical_and(slot >= 2, slot < 4))(lambda: back_conv(slot - 2, 1))
+            for hf in range(2):
+                plane_got(0, hf, 0)
+                plane_got(0, hf, 2)
+            tiles4(job3, z == 0)
+
+        @pl.when(jnp.logical_and(slot == 0, c == 0))
+        def _():
+            for hf in range(2):
+                plane_got(1, hf, 0)
+                plane_got(1, hf, 2)
+            tiles4(job2, jnp.logical_and(left2, z % 3 == 0))
 
         @pl.when(slot < 4)
         def _():
@@ -1278,27 +1341,69 @@
             for j in range(4):
                 recv_wait(g_block(1 - c, plane[j], slot), s.gfr.at[slot, j])
 
-        chain(0, slot, lambda q: own_down(0, q), True)
-        chain(1, slot, lambda q: own_down(1, q), True)
-
-        @pl.when(slot == LATE3)
+        job0(slot - (3 - z), z > 0)
+        job1(slot - jnp.where(z == 2, 1, 0), z != 1)
+        tap8(slot - 2 * (z % 3), jnp.logical_and(is_tap8, z != 2))
+
+        @pl.when(slot == 1)
         def _():
-            for j in (1, 2, 3):
-                for hf in range(2):
-                    recv_wait(half_of(s.pr3, j - 1, hf), s.pr.at[0, j - 1, hf])
-
-        chain(3, slot - LATE3, lambda q: own_plane(st3, s.pr3, q), False)
-
-        @pl.when(jnp.logical_and(slot == LATE2, has_plane2))
+            tiles4(job3, z == 1)
+            tiles4(job2, jnp.logical_and(left2, z == 1))
+
+        pl.when(slot == 2)(lambda: tiles4(job3, z == 2))
+
+        @pl.when(slot == 3)
         def _():
-            for j in (1, 2, 3):
-                for hf in range(2):
-                    recv_wait(half_of(s.pr2, j - 1, hf), s.pr.at[1, j - 1, hf])
-
-        chain(2, slot - jnp.where(is_tap8, 0, LATE2), own_two, is_tap8)
-        return 0
-
-    lax.fori_loop(0, 7 + max(LATE2 - 1, LATE3), step, 0)
+            halo_up_wait(7, s.G0.at[pl.ds(256, 128)])
+            lax.fori_loop(16, 24, shift_one, 0)
+            tiles4(job3, z == 3)
+
+        @pl.when(jnp.logical_and(slot == 3, c == 1))
+        def _():
+            for hf in range(2):
+                plane_second(1, hf)
+
+        pl.when(jnp.logical_and(slot >= 3, slot < 5))(lambda: back_conv(slot - 3, 1))
+
+        @pl.when(jnp.logical_and(slot == 4, c == 1))
+        def _():
+            for hf in range(2):
+                plane_got(1, hf, 0)
+                plane_got(1, hf, 2)
+            tiles4(job2, jnp.logical_and(late2, z % 3 == 0))
+
+        return 0
+
+    def job0(q, here):
+        chain(0, q, lambda q: own_down(0, q), put_down, here)
+
+    def job1(q, here):
+        chain(1, q, lambda q: own_down(1, q), put_down, here)
+
+    def tap8(q, here):
+        chain(2, q, lambda q: own_down(2, q), put_down, here)
+
+    def job2(q, here):
+        chain(2, q, lambda q: own_plane(s.st2, s.pr2, q), put_tile, here)
+
+    def job3(q, here):
+        chain(3, q, lambda q: own_plane(st3, s.pr3, q), put_tile, here)
+
+    def tiles4(job, here):
+        def body(q, _):
+            job(q, here)
+            return 0
+
+        @pl.when(here)
+        def _():
+            lax.fori_loop(0, 4, body, 0)
+
+    lax.fori_loop(0, 6, step, 0)
+    tiles4(job1, z == 1)
+    tiles4(job0, z == 0)
+    tiles4(job2, jnp.logical_and(late2, z == 1))
+    tiles4(job2, jnp.logical_and(has_plane2, z == 2))
+    tiles4(tap8, jnp.logical_and(is_tap8, z == 2))
     store(s.wgo, wg_ref)
     for i in range(4):
         store(s.inraw.at[i], ig_ref.at[:, i])
@@ -1310,16 +1415,12 @@
             g_direct(q, j).wait_send()
         for j in range(4):
             g_forward(q, j).wait_send()
-    for j in (1, 2, 3):
+    for job in range(2):
         for hf in range(2):
-            plane_copy(0, j, hf).wait_send()
-            pl.when(to_piece_owner(j))(lambda: plane_copy(1, j, hf).wait_send())
+            for m in range(3):
+                plane_sent(job, hf, m)
     for cp in outs:
         cp.wait()
-
-
-LATE3 = 1
-LATE2 = 4
 
 
 def hand_over(n, *refs):

time: 158 us -> 143 us (0.905)
  the two profiles are of different devices: /device:TPU:20 before, /device:TPU:17 now
where the time goes in v3:
time: 143 us
  Pallas kernels  142 us (99%)
  between operations  1.45 us (1%)
    pallas_call x1, Pallas kernels, fused_step(): pl.pallas_call(functools.partial(fused_kernel, names, 13, 8), out_shape=(...  139 us
    pallas_call x1, Pallas kernels, fused_step(): pl.pallas_call(functools.partial(hand_over, n), out_shape=tuple((sds(o.sh...  2.93 us

profile of v3, /device:TPU:17, one launch (start us, length us, event | category | flops | bytes accessed | tf_op | source)
XLA Modules:
  0.0 143.1 jit_solution(9073046770056529691)
XLA Ops:
  1.3 138.7 %shard_map.188 = (bf16[8,2,16,1024]{3,2,1,0:T(8,128)(2,1)}, bf16[8,2,16,512]{3,2,1,0:T(8,128)(2,1)}, bf16[8,4,32,512]{3,2,1,0:T(8,128)(2,1)}, f32[2048,128]{1,0:...) custom-call(bf16[8,4,32,512]{3,2,1,0:T(8,128)(2,1)} %refs_0_.1, ...), custom_call_target="tpu_custom_call" | custom-call | flops 12999999488 | bytes 21000000 | tf_op jit(solution)/shard_map/pallas_call | solution.py:1451
  140.0 2.9 %shard_map.189 = (bf16[8,2,16,1024]{3,2,1,0:T(8,128)(2,1)}, bf16[8,2,16,512]{3,2,1,0:T(8,128)(2,1)}, bf16[8,4,32,512]{3,2,1,0:T(8,128)(2,1)}, f32[2048,128]{1,0:...) custom-call(bf16[8,2,16,1024]{3,2,1,0:T(8,128)(2,1)} %get-tuple-element.24.refs_0_, ...), custom_call_target="tpu_custom_call" | custom-call | bytes 6000000 | tf_op jit(solution)/shard_map/pallas_call | solution.py:1477

commit v4 on v3

--- a/solution.py
+++ b/solution.py
@@ -535,7 +535,7 @@
         st[k][0:1, pl.ds(col, width)] = jnp.sum(t1, axis=0, keepdims=True)
         st[k][1:2, pl.ds(col, width)] = jnp.sum(t2, axis=0, keepdims=True)
 
-    def tiles(count_, body, init=0, unroll=2):
+    def rows_loop(count_, body, init=0, unroll=2):
         return lax.fori_loop(0, count_, body, init, unroll=unroll)
 
     def rows16(i):
@@ -660,7 +660,7 @@
         s.act1[rows16(i), :] = mish_of(zv).astype(BF)
         return 0
 
-    tiles(16, act_one)
+    rows_loop(16, act_one)
     loads["wl"].wait()
     loads["wr"].wait()
 
@@ -673,13 +673,14 @@
         s.yr[:, cols] = acc
         colstats(acc, 1, 512 + h * 256, 256)
     ar_send(1)
+    x_start((1, 2), (1,))
 
     def slope_one(i, _):
         zv = s.y1[rows16(i), :] * s.bn0[0:1, :] + s.bn0[1:2, :]
         s.d1[rows16(i), :] = mish_slope(zv)
         return 0
 
-    tiles(16, slope_one)
+    rows_loop(16, slope_one)
     mycols = pl.ds(al(c * 256, 256), 256)
 
     def xpose_act(h, _):
@@ -699,7 +700,6 @@
 
     cp_act = to_sib(s.J2X.at[pl.ds(2 - 2 * c, 2), :, mycols], s.J2X.at[pl.ds(2 * c, 2), :, mycols])
     cp_act.start()
-    x_start((1, 2), (1,))
 
     res = ar_recv(1)
     norm_params(1, res[:, 0:512], 1024, s.bnl, 512)
@@ -714,7 +714,7 @@
         s.dr[rows16(i), :] = t + 4.0 * zv * (e * (1.0 + e)) * (d * d)
         return 0
 
-    tiles(16, act_right)
+    rows_loop(16, act_right)
     loads["wm"].wait()
     for h in range(2):
         cols = pl.ds(h * 256, 256)
@@ -746,7 +746,7 @@
         return t1 + gz, t2 + gx
 
     zero16 = jnp.zeros((16, 512), F32)
-    t1, t2 = tiles(16, left_branch, (zero16, zero16), unroll=1)
+    t1, t2 = rows_loop(16, left_branch, (zero16, zero16), unroll=1)
     st[3][0:1, 512:1024] = jnp.sum(t1, axis=0, keepdims=True)
     st[3][1:2, 512:1024] = jnp.sum(t2, axis=0, keepdims=True)
     outs = []
@@ -788,7 +788,7 @@
         windows(i, mish_of(zv) * edge_at(i))
         return 0
 
-    tiles(32, act_mid)
+    rows_loop(32, act_mid)
     for i in range(3):
         loads["ws%d" % i].wait()
 
@@ -814,7 +814,7 @@
         s.dm[rows16(i), :] = mish_slope(zv)
         return 0
 
-    tiles(16, slope_mid)
+    rows_loop(16, slope_mid)
 
     def window_t(tap, dst, k):
         base = pl.ds(al((tap % 3) * 512 + (tap // 3) * 128, 128), 256)
@@ -869,7 +869,7 @@
         gx = gz * (yv * s.bn4[2:3, :] + s.bn4[3:4, :])
         return t1 + gz, t2 + gx
 
-    t1, t2 = tiles(16, norm_four, (zero16, zero16), unroll=1)
+    t1, t2 = rows_loop(16, norm_four, (zero16, zero16), unroll=1)
     st[4][0:1, :] = jnp.sum(t1, axis=0, keepdims=True)
     st[4][1:2, :] = jnp.sum(t2, axis=0, keepdims=True)
     ar_send(4)
@@ -883,7 +883,7 @@
         s.GA[pl.ds(al(c * 256 + i * 16, 16), 16), :] = val
         return 0
 
-    tiles(16, grad_left)
+    rows_loop(16, grad_left)
     cp_ga = to_sib(s.glb, s.GA.at[myrows])
 
     @pl.when(c == 1)
@@ -980,7 +980,7 @@
         s.g4[rows16(i), :] = mish_slope(zv) * (s.bc[i // 8, i % 8].astype(F32) * v)
         return 0
 
-    tiles(16, halo_four)
+    rows_loop(16, halo_four)
 
     res = ar_recv(4)
     back_params(res, 2560, s.bn4, 512)
@@ -990,7 +990,7 @@
         windows(i, grad_of(s.g4[rows16(i), :], s.y4[rows16(i), :], s.bn4, v).astype(BF).astype(F32))
         return 0
 
-    tiles(32, grad_four)
+    rows_loop(32, grad_four)
 
     def back_four(h, _):
         col = al(h * 256, 256)
@@ -1050,7 +1050,7 @@
         s.GB[pl.ds(al(c * 256 + i * 16, 16), 16), :] = val
         return 0
 
-    tiles(16, grad_mid)
+    rows_loop(16, grad_mid)
 
     def back_mid(h, _):
         col = al(h * 256, 256)
@@ -1082,7 +1082,7 @@
         cp_gb.start()
 
     for hf in range(2):
-        plane_start(0, hf, 0)
+        plane_second(0, hf)
     piece3(0)
     both_waits(cp_gb, 0)
 
@@ -1100,7 +1100,7 @@
 
         return 0
 
-    tiles(16, grad_right)
+    rows_loop(16, grad_right)
 
     def back_one(h, _):
         cols = pl.ds(al(h * 256, 256), 256)
@@ -1126,7 +1126,7 @@
         cp_gr.start()
 
     for hf in range(2):
-        plane_second(0, hf)
+        plane_start(0, hf, 0)
     both_waits(cp_gr, 0)
 
     @pl.when(c == 1)
@@ -1144,7 +1144,7 @@
         s.Gall[pl.ds(al(own8 * 256 + i * 16, 16), 16), :] = low
         return 0
 
-    tiles(16, grad_one)
+    rows_loop(16, grad_one)
 
     halo_up(7, s.G0.at[pl.ds(0, 128)], s.G0.at[pl.ds(256, 128)])
 
@@ -1324,14 +1324,14 @@
             for hf in range(2):
                 plane_got(0, hf, 0)
                 plane_got(0, hf, 2)
-            tiles4(job3, z == 0)
+            run_tiles(job3, z == 0, 0, 4)
 
         @pl.when(jnp.logical_and(slot == 0, c == 0))
         def _():
             for hf in range(2):
                 plane_got(1, hf, 0)
                 plane_got(1, hf, 2)
-            tiles4(job2, jnp.logical_and(left2, z % 3 == 0))
+            run_tiles(job2, jnp.logical_and(left2, z % 3 == 0), 0, 4)
 
         @pl.when(slot < 4)
         def _():
@@ -1342,21 +1342,16 @@
                 recv_wait(g_block(1 - c, plane[j], slot), s.gfr.at[slot, j])
 
         job0(slot - (3 - z), z > 0)
-        job1(slot - jnp.where(z == 2, 1, 0), z != 1)
-        tap8(slot - 2 * (z % 3), jnp.logical_and(is_tap8, z != 2))
-
-        @pl.when(slot == 1)
-        def _():
-            tiles4(job3, z == 1)
-            tiles4(job2, jnp.logical_and(left2, z == 1))
-
-        pl.when(slot == 2)(lambda: tiles4(job3, z == 2))
+        job1(slot - jnp.where(z == 0, 0, 4 - z), z != 1)
+        tap8(slot - 2 * z, jnp.logical_and(is_tap8, z < 2))
+        pl.when(jnp.logical_and(slot >= 1, slot < 3))(lambda: run_tiles(job3, z == 1, 2 * slot - 2, 2))
+        pl.when(jnp.logical_and(slot >= 3, slot < 5))(lambda: run_tiles(job3, z == 2, 2 * slot - 6, 2))
+        pl.when(slot == 3)(lambda: run_tiles(job2, jnp.logical_and(left2, z == 1), 0, 4))
 
         @pl.when(slot == 3)
         def _():
             halo_up_wait(7, s.G0.at[pl.ds(256, 128)])
             lax.fori_loop(16, 24, shift_one, 0)
-            tiles4(job3, z == 3)
 
         @pl.when(jnp.logical_and(slot == 3, c == 1))
         def _():
@@ -1370,7 +1365,7 @@
             for hf in range(2):
                 plane_got(1, hf, 0)
                 plane_got(1, hf, 2)
-            tiles4(job2, jnp.logical_and(late2, z % 3 == 0))
+            run_tiles(job2, jnp.logical_and(late2, z % 3 == 0), 0, 4)
 
         return 0
 
@@ -1389,21 +1384,23 @@
     def job3(q, here):
         chain(3, q, lambda q: own_plane(st3, s.pr3, q), put_tile, here)
 
-    def tiles4(job, here):
+    def run_tiles(job, here, first, n):
         def body(q, _):
-            job(q, here)
+            job(first + q, here)
             return 0
 
         @pl.when(here)
         def _():
-            lax.fori_loop(0, 4, body, 0)
+            lax.fori_loop(0, n, body, 0)
 
     lax.fori_loop(0, 6, step, 0)
-    tiles4(job1, z == 1)
-    tiles4(job0, z == 0)
-    tiles4(job2, jnp.logical_and(late2, z == 1))
-    tiles4(job2, jnp.logical_and(has_plane2, z == 2))
-    tiles4(tap8, jnp.logical_and(is_tap8, z == 2))
+    run_tiles(tap8, jnp.logical_and(is_tap8, z == 3), 0, 4)
+    run_tiles(job1, z == 1, 0, 4)
+    run_tiles(job0, z == 0, 0, 4)
+    run_tiles(job2, jnp.logical_and(late2, z == 1), 0, 4)
+    run_tiles(job3, z == 3, 0, 4)
+    run_tiles(job2, jnp.logical_and(has_plane2, z == 2), 0, 4)
+    run_tiles(tap8, jnp.logical_and(is_tap8, z == 2), 0, 4)
     store(s.wgo, wg_ref)
     for i in range(4):
         store(s.inraw.at[i], ig_ref.at[:, i])

time: 143 us -> 140 us (0.979)
  Pallas kernels: 142 us -> 138 us
    pallas_call x1, Pallas kernels: 139 us -> 135 us  [fused_step(): pl.pallas_call(functools.partial(fused_kernel, names, 13, 8), out_shape=(...]
where the time goes in v4:
time: 140 us
  Pallas kernels  138 us (99%)
  between operations  1.45 us (1%)
    pallas_call x1, Pallas kernels, fused_step(): pl.pallas_call(functools.partial(fused_kernel, names, 13, 8), out_shape=(...  135 us
    pallas_call x1, Pallas kernels, fused_step(): pl.pallas_call(functools.partial(hand_over, n), out_shape=tuple((sds(o.sh...  2.93 us

profile of v4, /device:TPU:17, one launch (start us, length us, event | category | flops | bytes accessed | tf_op | source)
XLA Modules:
  0.0 139.6 jit_solution(14324385742958804910)
XLA Ops:
  1.3 135.2 %shard_map.188 = (bf16[8,2,16,1024]{3,2,1,0:T(8,128)(2,1)}, bf16[8,2,16,512]{3,2,1,0:T(8,128)(2,1)}, bf16[8,4,32,512]{3,2,1,0:T(8,128)(2,1)}, f32[2048,128]{1,0:...) custom-call(bf16[8,4,32,512]{3,2,1,0:T(8,128)(2,1)} %refs_0_.1, ...), custom_call_target="tpu_custom_call" | custom-call | flops 12999999488 | bytes 21000000 | tf_op jit(solution)/shard_map/pallas_call | solution.py:1448
  136.5 2.9 %shard_map.189 = (bf16[8,2,16,1024]{3,2,1,0:T(8,128)(2,1)}, bf16[8,2,16,512]{3,2,1,0:T(8,128)(2,1)}, bf16[8,4,32,512]{3,2,1,0:T(8,128)(2,1)}, f32[2048,128]{1,0:...) custom-call(bf16[8,2,16,1024]{3,2,1,0:T(8,128)(2,1)} %get-tuple-element.24.refs_0_, ...), custom_call_target="tpu_custom_call" | custom-call | bytes 6000000 | tf_op jit(solution)/shard_map/pallas_call | solution.py:1474

commit v5 on v4

--- a/solution.py
+++ b/solution.py
@@ -1074,6 +1074,8 @@
 
     lax.fori_loop(0, 2, back_mid, 0)
     ar_send(6)
+    for hf in range(2):
+        plane_second(0, hf)
 
     cp_gb = to_sib(s.gm, s.GB.at[myrows])
 
@@ -1081,8 +1083,6 @@
     def _():
         cp_gb.start()
 
-    for hf in range(2):
-        plane_second(0, hf)
     piece3(0)
     both_waits(cp_gb, 0)
 
@@ -1114,6 +1114,8 @@
 
     lax.fori_loop(0, 4, back_one, 0)
     ar_send(7)
+    for hf in range(2):
+        plane_start(0, hf, 0)
 
     @pl.when(c == 1)
     def _():
@@ -1125,8 +1127,6 @@
     def _():
         cp_gr.start()
 
-    for hf in range(2):
-        plane_start(0, hf, 0)
     both_waits(cp_gr, 0)
 
     @pl.when(c == 1)
@@ -1394,6 +1394,8 @@
             lax.fori_loop(0, n, body, 0)
 
     lax.fori_loop(0, 6, step, 0)
+    for i in range(4):
+        store(s.inraw.at[i], ig_ref.at[:, i])
     run_tiles(tap8, jnp.logical_and(is_tap8, z == 3), 0, 4)
     run_tiles(job1, z == 1, 0, 4)
     run_tiles(job0, z == 0, 0, 4)
@@ -1402,8 +1404,6 @@
     run_tiles(job2, jnp.logical_and(has_plane2, z == 2), 0, 4)
     run_tiles(tap8, jnp.logical_and(is_tap8, z == 2), 0, 4)
     store(s.wgo, wg_ref)
-    for i in range(4):
-        store(s.inraw.at[i], ig_ref.at[:, i])
 
     for q in range(4):
         for zp in range(4):

time: 140 us -> 140 us (level)
  no operation moved by 1% of the time
where the time goes in v5:
time: 140 us; the launch traced here: 139 us
  Pallas kernels  138 us (99%)
  between operations  1.45 us (1%)
    pallas_call x1, Pallas kernels, fused_step(): pl.pallas_call(functools.partial(fused_kernel, names, 13, 8), out_shape=(...  135 us
    pallas_call x1, Pallas kernels, fused_step(): pl.pallas_call(functools.partial(hand_over, n), out_shape=tuple((sds(o.sh...  2.93 us

profile of v5, /device:TPU:17, one launch (start us, length us, event | category | flops | bytes accessed | tf_op | source)
XLA Modules:
  0.0 139.3 jit_solution(14986228610807532014)
XLA Ops:
  1.3 134.9 %shard_map.188 = (bf16[8,2,16,1024]{3,2,1,0:T(8,128)(2,1)}, bf16[8,2,16,512]{3,2,1,0:T(8,128)(2,1)}, bf16[8,4,32,512]{3,2,1,0:T(8,128)(2,1)}, f32[2048,128]{1,0:...) custom-call(bf16[8,4,32,512]{3,2,1,0:T(8,128)(2,1)} %refs_0_.1, ...), custom_call_target="tpu_custom_call" | custom-call | flops 12999999488 | bytes 21000000 | tf_op jit(solution)/shard_map/pallas_call | solution.py:1448
  136.2 2.9 %shard_map.189 = (bf16[8,2,16,1024]{3,2,1,0:T(8,128)(2,1)}, bf16[8,2,16,512]{3,2,1,0:T(8,128)(2,1)}, bf16[8,4,32,512]{3,2,1,0:T(8,128)(2,1)}, f32[2048,128]{1,0:...) custom-call(bf16[8,2,16,1024]{3,2,1,0:T(8,128)(2,1)} %get-tuple-element.24.refs_0_, ...), custom_call_target="tpu_custom_call" | custom-call | bytes 6000000 | tf_op jit(solution)/shard_map/pallas_call | solution.py:1474
